TPU v7x, 256 devices: a whole 4x4x8 slice. The times are simulated.
256 devices in a mesh: snp: 32 (over y, z), ind: 8 (over x, core).
Axes of the slice: x: 4, y: 4, z: 8, core: 2. Of those that a mesh axis runs over, the one named last changes fastest.
Arguments:
- beta_hat: float32 [64, 32768], P('ind', 'snp'), may hold values from -8 to 8
- ld_band: float32 [32768, 1024], P('snp'), as said below
- band_start: int32 [256], P('snp'), may hold values from -480 to 32224, as said below
- heritability: float32 [64], P('ind'), may hold values from 0.2 to 0.6
- genotypes: bfloat16 [8192, 32768], P('ind', 'snp'), may hold values from 0 to 2, as said below
Outputs:
- weights: float32 [64, 32768], P('ind', 'snp')
- scores: float32 [64, 8192], P(None, ('ind', 'snp'))
Inputs may be any that keep to these rules, and one draw needn't show every extreme that they name: ld_band is a symmetric matrix R in band form: entry k of row i is R[i, band_start[i // 128] + k]; R[i, i] = 1; R[i, j] = 0 when |i - j| > 416 or j lies outside the SNPs; the off-diagonal magnitudes of a row sum to 2.5 at most. `band_start`: block b's window starts at 128 * b - 416 - k with k from 0 to 64; the first block has k = 64 and the last block k = 0. `genotypes`: dosages are 0, 1 or 2.
All inputs are finite; a program needn't handle non-finite values.
Results may differ from a plain program's by a relative error of at most 0.0021.
Values may be sent and summed in bfloat16 or wider, within the bound.
A program may use at most 64 MiB of HBM per device.

v0:
```python
import jax
import jax.numpy as jnp
from jax import lax
from jax.sharding import PartitionSpec as P

BLK = 128
ITERS = 2
M_GENOME = 1100000
N_GWAS = 1000000


def padded_2(block, sides, width):
    for axis, dim in sides:
        count = lax.axis_size(axis)
        forward = [(i, i + 1) for i in range(count - 1)]
        backward = [(target, source) for source, target in forward]
        low = lax.ppermute(
            lax.slice_in_dim(block, block.shape[dim] - width, None, axis=dim), axis, forward
        )
        high = lax.ppermute(lax.slice_in_dim(block, 0, width, axis=dim), axis, backward)
        block = jnp.concatenate([low, block, high], axis=dim)
    return block


def apply_operator(vector, ld_band, band_start, ridge_shift):
    band_cols = ld_band.shape[1]
    halo_cols = band_cols - BLK
    padded = padded_2(vector, (("snp", 1),), halo_cols)
    local_rows = vector.shape[1]
    offsets = band_start - lax.axis_index("snp") * local_rows + halo_cols
    windows = jax.vmap(lambda row_begin: lax.dynamic_slice_in_dim(padded, row_begin, band_cols, 1))(
        offsets
    )
    blocks = ld_band.reshape(band_start.shape[0], BLK, band_cols)
    product = jnp.einsum("btk,brk->tbr", windows, blocks, precision=lax.Precision.HIGHEST)
    return product.reshape(vector.shape) + ridge_shift[:, None] * vector


def norm_sum(residual):
    return lax.psum(jnp.sum(residual * residual, axis=1), "snp")


def local(beta_hat, ld_band, band_start, heritability, genotypes):
    ridge_shift = M_GENOME / N_GWAS / heritability
    weights = jnp.zeros_like(beta_hat)
    residual = beta_hat
    direction = beta_hat
    norm_now = norm_sum(residual)
    for turn_index in range(ITERS):
        product = apply_operator(direction, ld_band, band_start, ridge_shift)
        curved = lax.psum(jnp.sum(direction * product, axis=1), "snp")
        step_size = norm_now / curved
        weights = weights + step_size[:, None] * direction
        residual = residual - step_size[:, None] * product
        if turn_index + 1 < ITERS:
            norm_next = norm_sum(residual)
            direction = residual + (norm_next / norm_now)[:, None] * direction
            norm_now = norm_next
    rounded = weights.astype(jnp.bfloat16)
    partial_scores = lax.dot_general(
        lax.all_gather(rounded, "ind", axis=0, tiled=True),
        genotypes,
        (((1,), (1,)), ((), ())),
        preferred_element_type=jnp.float32,
    )
    complete = lax.psum(partial_scores, "snp")
    count = complete.shape[1] * lax.axis_size("ind")
    summed = lax.psum(jnp.sum(complete, axis=1), "ind")
    average = summed / count
    centred = complete - average[:, None]
    variance = lax.psum(jnp.sum(centred * centred, axis=1), "ind") / count
    share_cols = complete.shape[1] // lax.axis_size("snp")
    own_part = lax.dynamic_slice_in_dim(centred, lax.axis_index("snp") * share_cols, share_cols, 1)
    scores = own_part * lax.rsqrt(variance + 1e-05)[:, None]
    return (weights, scores)


def solution(mesh):
    placed = (P("ind", "snp"), P("snp", None), P("snp"), P("ind"), P("ind", "snp"))
    return jax.shard_map(
        local,
        mesh=mesh,
        in_specs=placed,
        out_specs=(P("ind", "snp"), P(None, ("ind", "snp"))),
        check_vma=False,
    )
```

profile of v0, /device:TPU:1, one launch (start us, length us, event | category | flops | bytes accessed | tf_op | source)
XLA Modules:
  0.0 465.0 jit_solution(3514487914134571717)
XLA Ops:
  7.2 0.9 fusion.7
  8.1 4.4 collective-permute-start
  12.5 1.3 collective-permute-start.1
  15.2 2.2 collective-permute-done.1
  17.3 0.8 pad_maximum_fusion
  18.1 10.5 %while.2 = (s32[]{:T(128)}, f32[8,2816]{1,0:T(8,128)S(1)}, s32[8,2]{0,1:T(2,128)S(1)}, f32[8,8,1024]{2,1,0:T(8,128)S(1)}, s32[]{:T(128)}) while((s32[]{:T(128)}, f32[8,2816]{1,0:T(8,128)S(1)}, s32[8,2]{0,1:T(2,128)S(1)}, f32[8,8,1024]{2,1,0:T(8,128)S(1)}, s32[]{:T(128)}) %tuple.38), condition=%wide.while_cond, body=%wide.while_body.sunk | while | flops 2 | bytes 65633 | solution.py:31
  18.7 0.7 bitcast_dynamic-update-slice_fusion.4
  20.0 0.7 bitcast_dynamic-update-slice_fusion.4
  28.6 5.4 %multiply_reduce_fusion.2 = (f32[8]{0:T(128)S(1)}, f32[8]{0:T(128)S(1)}, f32[8,1024]{1,0:T(8,128)S(1)}) fusion(f32[8,1024]{1,0:T(8,128)} %param.5, f32[8]{0:T(128)S(1)} %broadcast_divide_fusion, f32[8,8,1024]{2,1,0:T(8,128)S(1)} %get-tuple-element.9, f32[8,128,1024]{2,1,0:T(8,128)} %bitcast.39), kind=kOutput, calls=%fused_computation.19 | convolution fusion | flops 100712432 | bytes 4522080 | tf_op jit(solution)/shard_map/btk,brk->tbr/dot_general | solution.py:35
  34.1 62.4 %all-reduce.1 = (f32[8]{0:T(128)S(1)}, f32[8]{0:T(128)S(1)}) all-reduce(f32[8]{0:T(128)S(1)} %get-tuple-element.21, f32[8]{0:T(128)S(1)} %get-tuple-element.20), channel_id=1, replica_groups=mesh['snp'=32,'ind'=8] {'snp'}, use_global_device_ids=true, to_apply=%region_1.0 | all-reduce | flops 16 | bytes 128 | tf_op jit(solution)/shard_map/psum | solution.py:40
  96.6 55.7 %psum.51 = f32[8]{0:T(128)S(1)} all-reduce(f32[8]{0:T(128)S(1)} %multiply_reduce_fusion.1), channel_id=1, replica_groups=mesh['snp'=32,'ind'=8] {'snp'}, use_global_device_ids=true, to_apply=%region_5.0 | all-reduce | flops 8 | bytes 64 | tf_op jit(solution)/shard_map/psum | solution.py:40
  152.5 3.6 collective-permute-start.2
  156.0 1.3 collective-permute-start.3
  157.3 3.6 collective-permute-done.3
  161.0 10.5 %while.3 = (s32[]{:T(128)}, f32[8,2816]{1,0:T(8,128)S(1)}, s32[8,2]{0,1:T(2,128)S(1)}, f32[8,8,1024]{2,1,0:T(8,128)S(1)}, s32[]{:T(128)}) while((s32[]{:T(128)}, f32[8,2816]{1,0:T(8,128)S(1)}, s32[8,2]{0,1:T(2,128)S(1)}, f32[8,8,1024]{2,1,0:T(8,128)S(1)}, s32[]{:T(128)}) %tuple.46), condition=%wide.while_cond.1, body=%wide.while_body.1.sunk | while | flops 2 | bytes 65633 | solution.py:31
  171.5 5.4 %fusion.3 = f32[8]{0:T(128)S(1)} fusion(f32[8,1024]{1,0:T(8,128)S(1)} %multiply_add_fusion.1, f32[8,8,1024]{2,1,0:T(8,128)S(1)} %get-tuple-element.17, f32[8,128,1024]{2,1,0:T(8,128)} %bitcast.40, f32[8]{0:T(128)S(1)} %broadcast_divide_fusion), kind=kOutput, calls=%fused_computation.9 | convolution fusion | flops 100696056 | bytes 4489280 | tf_op jit(solution)/shard_map/btk,brk->tbr/dot_general | solution.py:35
  176.9 55.7 %psum.52 = f32[8]{0:T(128)S(1)} all-reduce(f32[8]{0:T(128)S(1)} %fusion.3), channel_id=1, replica_groups=mesh['snp'=32,'ind'=8] {'snp'}, use_global_device_ids=true, to_apply=%region_7.0 | all-reduce | flops 8 | bytes 64 | tf_op jit(solution)/shard_map/psum | solution.py:51
  233.3 57.2 %all_gather.3 = bf16[64,1024]{1,0:T(8,128)(2,1)S(1)} all-gather(bf16[8,1024]{1,0:T(8,128)(2,1)S(1)} %get-tuple-element.42), channel_id=1, replica_groups=mesh['snp'=32,'ind'=8] {'ind'}, dimensions={0}, use_global_device_ids=true | all-gather | bytes 147456 | tf_op jit(solution)/shard_map/all_gather | solution.py:61
  290.5 1.5 fusion.8
  292.0 133.9 %all-reduce.4.cloned.1.call-done = f32[64,1024]{1,0:T(8,128)} async-done(((f32[64,1024]{1,0:T(8,128)}), f32[64,1024]{1,0:T(8,128)}) %all-reduce.4.cloned.1.call-update) | async-done | bytes 262160 | tf_op jit(solution)/shard_map/psum | solution.py:66
  425.9 1.1 reduce_sum.58
  426.9 16.9 %psum.54 = f32[64]{0:T(128)S(1)} all-reduce(f32[64]{0:T(128)S(1)} %reduce_sum.58), channel_id=1, replica_groups=mesh['snp'=32,'ind'=8] {'ind'}, use_global_device_ids=true, to_apply=%region_10.0 | all-reduce | flops 64 | bytes 512 | tf_op jit(solution)/shard_map/psum | solution.py:68
  443.8 1.1 multiply_reduce_fusion
  445.0 12.4 %psum.55 = f32[64]{0:T(128)S(1)} all-reduce(f32[64]{0:T(128)S(1)} %get-tuple-element.40), channel_id=1, replica_groups=mesh['snp'=32,'ind'=8] {'ind'}, use_global_device_ids=true, to_apply=%region_12.0 | all-reduce | flops 64 | bytes 512 | tf_op jit(solution)/shard_map/psum | solution.py:71
  (71 shorter events, 22.8 us)
Async XLA Ops:
  7.2 283.4 %copy-start = (bf16[1024,1024]{1,0:T(8,128)(2,1)S(1)}, bf16[1024,1024]{1,0:T(8,128)(2,1)}, u32[]{:S(2)}) copy-start(bf16[1024,1024]{1,0:T(8,128)(2,1)} %param.9) | copy-start | bytes 6291460
  7.2 89.3 %copy-start.1 = (f32[8,1024]{1,0:T(8,128)S(1)}, f32[8,1024]{1,0:T(8,128)}, u32[]{:S(2)}) copy-start(f32[8,1024]{1,0:T(8,128)} %param.5) | copy-start | bytes 98308
  7.2 418.7 %all-reduce.4.cloned.1.call-start = ((), (), s32[]{:S(2)}) async-start(), calls=%async_computation | async-start | bytes 524288 | tf_op jit(solution)/shard_map/psum | solution.py:66
  8.1 7.0 %collective-permute-start = (f32[8,896]{1,0:T(8,128)S(1)}, f32[8,896]{1,0:T(8,128)S(1)}, u32[]{:S(2)}, u32[]{:S(2)}) collective-permute-start(f32[8,896]{1,0:T(8,128)S(1)} %get-tuple-element.46), channel_id=1, source_target_pairs={{0,8},{8,16},{16,24},{24,32},{32,40},{40,48},{48,56},{56,64},{64,7... | collective-permute-start | bytes 86024 | tf_op jit(solution)/shard_map/ppermute | solution.py:17
  12.5 4.8 %collective-permute-start.1 = (f32[8,896]{1,0:T(8,128)S(1)}, f32[8,896]{1,0:T(8,128)S(1)}, u32[]{:S(2)}, u32[]{:S(2)}) collective-permute-start(f32[8,896]{1,0:T(8,128)S(1)} %get-tuple-element.47), channel_id=1, source_target_pairs={{8,0},{16,8},{24,16},{32,24},{40,32},{48,40},{56,48},{64,56},{72,6... | collective-permute-start | bytes 86024 | tf_op jit(solution)/shard_map/ppermute | solution.py:20
  152.5 4.9 %collective-permute-start.2 = (f32[8,896]{1,0:T(8,128)S(1)}, f32[8,896]{1,0:T(8,128)S(1)}, u32[]{:S(2)}, u32[]{:S(2)}) collective-permute-start(f32[8,896]{1,0:T(8,128)S(1)} %get-tuple-element.44), channel_id=1, source_target_pairs={{0,8},{8,16},{16,24},{24,32},{32,40},{40,48},{48,56},{56,64},{64,7... | collective-permute-start | bytes 86024 | tf_op jit(solution)/shard_map/ppermute | solution.py:17
  156.0 4.9 %collective-permute-start.3 = (f32[8,896]{1,0:T(8,128)S(1)}, f32[8,896]{1,0:T(8,128)S(1)}, u32[]{:S(2)}, u32[]{:S(2)}) collective-permute-start(f32[8,896]{1,0:T(8,128)S(1)} %get-tuple-element.45), channel_id=1, source_target_pairs={{8,0},{16,8},{24,16},{32,24},{40,32},{48,40},{56,48},{64,56},{72,6... | collective-permute-start | bytes 86024 | tf_op jit(solution)/shard_map/ppermute | solution.py:20
Sparse Core Ops, SparseCore 0:
  292.1 133.6 all-reduce.3
where the time goes:
time: 466 us; the launch traced here: 465 us
  blocking collectives  260 us (56%)
  waiting for transfers between devices  140 us (30%)
  local copies, waits for them, and re-layouts  22.7 us (5%)
  between operations  14.1 us (3%)
  matrix products  12.3 us (3%)
  starting transfers between devices  10.5 us (2%)
  other arithmetic  5.4 us (1%)
    psum x1, waiting for transfers between devices, local(): complete = lax.psum(partial_scores, 'snp')  134 us
    psum x2, blocking collectives, norm_sum(): return lax.psum(jnp.sum(residual * residual, axis=1), 'snp')  118 us
    all_gather x1, blocking collectives, local(): lax.all_gather(rounded, 'ind', axis=0, tiled=True)  57.2 us
    psum x1, blocking collectives, local(): curved = lax.psum(jnp.sum(direction * product, axis=1), 'snp')  55.7 us
    gather x48, local copies, waits for them, and re-layouts  21 us
    psum x1, blocking collectives, local(): summed = lax.psum(jnp.sum(complete, axis=1), 'ind')  16.9 us
    psum x1, blocking collectives, local(): variance = lax.psum(jnp.sum(centred * centred, axis=1), 'ind') / count  12.4 us
    dot_general x2, matrix products, apply_operator(): jnp.einsum('btk,brk->tbr', windows, blocks, precision=lax.Precision.HIGHEST)  10.8 us
  transfers between devices with their start and end apart: 5, of which 3 were waited for; matrix products, arithmetic and copies ran while one was open for 0% of the time, Pallas kernels for 0%

commit v1 on v0

v1 whole, which is shorter than its diff:
```python
import functools

import jax
import jax.numpy as jnp
from jax import lax
from jax.experimental import pallas as pl
from jax.experimental.pallas import tpu as pltpu
from jax.sharding import PartitionSpec as P

BLK = 128
M_GENOME = 1100000
N_GWAS = 1000000
SNP, IND = 32, 8
Y, Z, X = 4, 8, 4
NB = 8
TR = 8
COLS = NB * BLK
HALO = 512
SPAN = 1152
SHARE = 32
MESH = pl.DeviceIdType.MESH
NT = (((1,), (1,)), ((), ()))
F32, BF16 = jnp.float32, jnp.bfloat16


def ring(n):
    return sorted(range(n), key=lambda k: -min(k, n - k))


SNP_OFFSETS = sorted(
    ((a, b) for a in range(Y) for b in range(Z) if (a, b) != (0, 0)),
    key=lambda q: -(min(q[0], Y - q[0]) + min(q[1], Z - q[1])),
)
IND_OFFSETS = [(a, c) for a in ring(X) for c in (1, 0) if (a, c) != (0, 0)]


def split(value):
    high = value.astype(BF16).astype(F32)
    return jnp.concatenate([high, value - high], axis=0).astype(BF16)


def fold(out):
    return out[0:8, 0:BLK] + out[8:16, 0:BLK] + out[0:8, BLK:] + out[8:16, BLK:]


def local_part(vec, hilo, acc):
    for b in range(NB):
        own0, own1 = max(0, BLK * b - HALO), min(COLS, BLK * b + SPAN - HALO)
        k0 = own0 + HALO - BLK * b
        out = lax.dot_general(
            vec[:, own0:own1], hilo[b, :, k0 : k0 + own1 - own0], NT, preferred_element_type=F32
        )
        acc[:, b * BLK : (b + 1) * BLK] = fold(out)


def halo_part(left, right, hilo, acc):
    for b in range(NB):
        if b < 4:
            vec, k0, k1 = left[:, BLK * b :], 0, HALO - BLK * b
        else:
            vec, k0, k1 = right[:, : BLK * (b - 3)], HALO + COLS - BLK * b, SPAN
        out = lax.dot_general(vec, hilo[b, :, k0:k1], NT, preferred_element_type=F32)
        acc[:, b * BLK : (b + 1) * BLK] += fold(out)


def wait_for(ref, sem):
    pltpu.make_async_copy(ref, ref, sem).wait()


def lane_sum(value):
    return jnp.sum(value, axis=1, keepdims=True)


def kernel(
    start_ref,
    herit_ref,
    beta_ref,
    ld_ref,
    geno_ref,
    weights_ref,
    scores_ref,
    ldbuf,
    hilo,
    geno,
    acc,
    ubuf,
    halo,
    mom_own,
    mom_in,
    wall,
    part,
    part_in,
    stat_own,
    stat_in,
    stat_own2,
    stat_in2,
    ld_sem,
    geno_sem,
    halo_send,
    halo_recv,
    send_sem,
    recv_sem,
):
    s, i = lax.axis_index("snp"), lax.axis_index("ind")
    y, z, x, core = s // Z, s % Z, i // 2, i % 2

    def snp_peer(dy, dz):
        return lax.rem(y + dy, Y) * Z + lax.rem(z + dz, Z)

    def ind_peer(dx, dc):
        return lax.rem(x + dx, X) * 2 + lax.rem(core + dc, 2)

    def load(b):
        return pltpu.make_async_copy(ld_ref.at[pl.ds(b * BLK, BLK)], ldbuf.at[b], ld_sem.at[b])

    for b in range(NB):
        load(b).start()
    load_geno = pltpu.make_async_copy(geno_ref, geno, geno_sem)
    load_geno.start()

    barrier = pltpu.get_barrier_semaphore()
    for dy, dz in SNP_OFFSETS:
        pl.semaphore_signal(barrier, inc=1, device_id=(snp_peer(dy, dz), i), device_id_type=MESH)
    for dx, dc in IND_OFFSETS:
        pl.semaphore_signal(barrier, inc=1, device_id=(s, ind_peer(dx, dc)), device_id_type=MESH)
    pl.semaphore_wait(barrier, len(SNP_OFFSETS) + len(IND_OFFSETS))

    right, left = lax.rem(s + 1, SNP), lax.rem(s + SNP - 1, SNP)

    def send_halo(src, turn):
        copies = [
            pltpu.make_async_remote_copy(
                src_ref=src.at[:, COLS - HALO :],
                dst_ref=halo.at[turn, 0],
                send_sem=halo_send.at[turn, 0],
                recv_sem=halo_recv.at[turn, 0],
                device_id=(right, i),
                device_id_type=MESH,
            ),
            pltpu.make_async_remote_copy(
                src_ref=src.at[:, :HALO],
                dst_ref=halo.at[turn, 1],
                send_sem=halo_send.at[turn, 1],
                recv_sem=halo_recv.at[turn, 1],
                device_id=(left, i),
                device_id_type=MESH,
            ),
        ]
        for copy in copies:
            copy.start()
        return copies

    halo0 = send_halo(beta_ref, 0)

    for b in range(NB):
        load(b).wait()
        shift = start_ref[b] - (BLK * (s * NB + b) - HALO)

        def rows(k, carry, b=b, shift=shift):
            r0 = pl.multiple_of(k * 32, 32)
            value = ldbuf[b, pl.ds(r0, 32), :]
            value = jnp.concatenate([value, jnp.zeros((32, SPAN - COLS), F32)], axis=1)
            value = pltpu.roll(value, shift, 1)
            high = value.astype(BF16)
            hilo[b, pl.ds(r0, 32), :] = high
            hilo[b, pl.ds(BLK + r0, 32), :] = (value - high.astype(F32)).astype(BF16)
            return carry

        lax.fori_loop(0, BLK // 32, rows, 0)

    def off_diagonal(value, turn, copies):
        parts = split(value)
        local_part(parts, hilo, acc)
        for copy in copies:
            copy.wait_recv()
        halo_part(split(halo[turn, 0]), split(halo[turn, 1]), hilo, acc)
        return acc[...] - (parts[0:8].astype(F32) + parts[8:16].astype(F32))

    beta = beta_ref[...]
    u = off_diagonal(beta, 0, halo0)
    ubuf[...] = u
    halo1 = send_halo(ubuf, 1)

    p0 = lane_sum(beta * beta)
    p1 = lane_sum(beta * u)
    theta = jnp.where(p0 > 0, p1 / p0, 0.0)
    e = u - theta * beta
    q = lane_sum(e * e)
    t = lane_sum(e * beta)
    g = off_diagonal(u, 1, halo1) - theta * u
    f = lane_sum(e * g)
    h = lane_sum(beta * g)

    lane = lax.broadcasted_iota(jnp.int32, (TR, BLK), 1)
    tile = jnp.broadcast_to(p0, (TR, BLK))
    for k, value in enumerate((theta, q, t, f, h)):
        tile = jnp.where(lane >= 16 * (k + 1), value, tile)
    mom_own[...] = tile
    mom_in[len(SNP_OFFSETS)] = tile
    for j, (dy, dz) in enumerate(SNP_OFFSETS):
        pltpu.make_async_remote_copy(
            src_ref=mom_own,
            dst_ref=mom_in.at[j],
            send_sem=send_sem.at[0],
            recv_sem=recv_sem.at[0],
            device_id=(snp_peer(dy, dz), i),
            device_id_type=MESH,
        ).start()

    row = lax.broadcasted_iota(jnp.int32, (TR, 1), 0)
    herit = jnp.zeros((TR, 1), F32)
    for k in range(TR):
        herit = jnp.where(row == k, herit_ref[k], herit)
    kappa = 1.0 + (M_GENOME / N_GWAS) / herit

    wait_for(mom_in.at[0 : len(SNP_OFFSETS)], recv_sem.at[0])
    p0_d, th_d, q_d, t_d, f_d, h_d = [mom_in[:, :, 16 * k : 16 * k + 1] for k in range(6)]
    p0 = jnp.sum(p0_d, axis=0)
    theta = jnp.sum(p0_d * th_d + t_d, axis=0) / p0
    delta = th_d - theta[None]
    q = jnp.sum(q_d + delta * (2.0 * t_d + delta * p0_d), axis=0)
    t = jnp.sum(t_d + delta * p0_d, axis=0)
    f = jnp.sum(
        f_d + delta * (q_d + th_d * t_d + h_d + delta * (t_d + th_d * p0_d)), axis=0
    )
    a11 = p0 * (theta + kappa)
    a12 = q + (theta + kappa) * t
    a22 = f + kappa * q
    det = a11 * a22 - a12 * a12
    c1 = jnp.where(det > 0, (t * a11 - p0 * a12) / det, 0.0)
    c0 = (p0 - c1 * a12) / a11
    weights = (c0 - c1 * theta) * beta + c1 * u
    weights_ref[...] = weights

    wall[i] = jnp.concatenate([weights[:, 0:HALO], weights[:, HALO:]], axis=0).astype(BF16)
    for dx, dc in IND_OFFSETS:
        pltpu.make_async_remote_copy(
            src_ref=wall.at[i],
            dst_ref=wall.at[i],
            send_sem=send_sem.at[1],
            recv_sem=recv_sem.at[1],
            device_id=(s, ind_peer(dx, dc)),
            device_id_type=MESH,
        ).start()
    load_geno.wait()
    wait_for(wall.at[0 : len(IND_OFFSETS)], recv_sem.at[1])
    every = wall[...].astype(F32)
    rounded = jnp.concatenate(
        [every[:, 0:8].reshape(64, HALO), every[:, 8:16].reshape(64, HALO)], axis=1
    ).astype(BF16)

    slot = {offset: j for j, offset in enumerate(SNP_OFFSETS)}
    for dy in ring(Y):
        group = lax.rem(y + dy, Y)
        rows = geno[pl.ds(pl.multiple_of(group * 256, 256), 256), :]
        out = lax.dot_general(rows, rounded, NT, preferred_element_type=F32).reshape(Z, 2, 16, 64)
        part[pl.ds(group * Z, Z)] = jnp.concatenate([out[:, 0], out[:, 1]], axis=2)
        for dz in ring(Z):
            if (dy, dz) != (0, 0):
                peer = group * Z + lax.rem(z + dz, Z)
                pltpu.make_async_remote_copy(
                    src_ref=part.at[peer],
                    dst_ref=part_in.at[slot[dy, dz]],
                    send_sem=send_sem.at[2],
                    recv_sem=recv_sem.at[2],
                    device_id=(peer, i),
                    device_id_type=MESH,
                ).start()
    own = part[s]
    wait_for(part_in, recv_sem.at[2])
    raw = own + jnp.sum(part_in[...], axis=0)

    half = lax.broadcasted_iota(jnp.int32, (1, BLK), 1) < 64

    def both(value):
        return value + pltpu.roll(value, 64, 1)

    mean = both(jnp.sum(raw, axis=0, keepdims=True)) * (1.0 / SHARE)
    spread = both(jnp.sum((raw - mean) * (raw - mean), axis=0, keepdims=True))
    stat = jnp.where(half, mean, spread)

    def merge(values, count, size):
        total = jnp.sum(values, axis=0)
        mean = total * (1.0 / count)
        apart = jnp.where(half, values - mean, 0.0)
        squares = jnp.sum(apart * apart, axis=0) * float(size)
        return jnp.where(half, mean, total + pltpu.roll(squares, 64, 1))

    stat_own[...] = stat
    stat_in[len(SNP_OFFSETS)] = stat
    for j, (dy, dz) in enumerate(SNP_OFFSETS):
        pltpu.make_async_remote_copy(
            src_ref=stat_own,
            dst_ref=stat_in.at[j],
            send_sem=send_sem.at[3],
            recv_sem=recv_sem.at[3],
            device_id=(snp_peer(dy, dz), i),
            device_id_type=MESH,
        ).start()
    wait_for(stat_in.at[0 : len(SNP_OFFSETS)], recv_sem.at[3])
    stat = merge(stat_in[...], SNP, SHARE)
    stat_own2[...] = stat
    stat_in2[len(IND_OFFSETS)] = stat
    for j, (dx, dc) in enumerate(IND_OFFSETS):
        pltpu.make_async_remote_copy(
            src_ref=stat_own2,
            dst_ref=stat_in2.at[j],
            send_sem=send_sem.at[4],
            recv_sem=recv_sem.at[4],
            device_id=(s, ind_peer(dx, dc)),
            device_id_type=MESH,
        ).start()
    wait_for(stat_in2.at[0 : len(IND_OFFSETS)], recv_sem.at[4])
    stat = merge(stat_in2[...], IND, SHARE * SNP)
    swapped = pltpu.roll(stat, 64, 1)
    mean = jnp.where(half, stat, swapped)
    variance = jnp.where(half, swapped, stat) * (1.0 / (SHARE * SNP * IND))
    scores = (raw - mean) * lax.rsqrt(variance + 1e-05)
    scores_ref[0:16, :] = scores[:, 0:64]
    scores_ref[16:32, :] = scores[:, 64:128]

    for copy in halo0 + halo1:
        copy.wait_send()
    wait_for(mom_in.at[0 : len(SNP_OFFSETS)], send_sem.at[0])
    wait_for(wall.at[0 : len(IND_OFFSETS)], send_sem.at[1])
    wait_for(part_in, send_sem.at[2])
    wait_for(stat_in.at[0 : len(SNP_OFFSETS)], send_sem.at[3])
    wait_for(stat_in2.at[0 : len(IND_OFFSETS)], send_sem.at[4])


def local(beta_hat, ld_band, band_start, heritability, genotypes):
    vmem, smem = pl.BlockSpec(memory_space=pltpu.VMEM), pl.BlockSpec(memory_space=pltpu.SMEM)
    anywhere = pl.BlockSpec(memory_space=pl.ANY)
    dma = pltpu.SemaphoreType.DMA
    weights, scores = pl.pallas_call(
        kernel,
        out_shape=(
            jax.ShapeDtypeStruct((TR, COLS), F32),
            jax.ShapeDtypeStruct((SHARE, 64), F32),
        ),
        in_specs=[smem, smem, vmem, anywhere, anywhere],
        out_specs=(vmem, vmem),
        scratch_shapes=[
            pltpu.VMEM((NB, BLK, COLS), F32),
            pltpu.VMEM((NB, 2 * BLK, SPAN), BF16),
            pltpu.VMEM((1024, COLS), BF16),
            pltpu.VMEM((TR, COLS), F32),
            pltpu.VMEM((TR, COLS), F32),
            pltpu.VMEM((2, 2, TR, HALO), F32),
            pltpu.VMEM((TR, BLK), F32),
            pltpu.VMEM((SNP, TR, BLK), F32),
            pltpu.VMEM((IND, 16, HALO), BF16),
            pltpu.VMEM((SNP, 16, BLK), F32),
            pltpu.VMEM((SNP - 1, 16, BLK), F32),
            pltpu.VMEM((1, BLK), F32),
            pltpu.VMEM((SNP, 1, BLK), F32),
            pltpu.VMEM((1, BLK), F32),
            pltpu.VMEM((IND, 1, BLK), F32),
            dma((NB,)),
            dma,
            dma((2, 2)),
            dma((2, 2)),
            dma((5,)),
            dma((5,)),
        ],
        name="ldpred_scores",
        compiler_params=pltpu.CompilerParams(
            collective_id=0, has_side_effects=True, vmem_limit_bytes=40 << 20
        ),
    )(band_start, heritability, beta_hat, ld_band, genotypes)
    return weights, scores.T


def solution(mesh):
    placed = (P("ind", "snp"), P("snp", None), P("snp"), P("ind"), P("ind", "snp"))
    return jax.shard_map(
        local,
        mesh=mesh,
        in_specs=placed,
        out_specs=(P("ind", "snp"), P(None, ("ind", "snp"))),
        check_vma=False,
    )
```

time: 466 us -> 60 us (0.13)
  blocking collectives: 260 us -> 0 us
  waiting for transfers between devices: 140 us -> 0 us
  Pallas kernels: 0 us -> 52 us
  local copies, waits for them, and re-layouts: 22.7 us -> 7.06 us
  between operations: 14.1 us -> 0.65 us
  matrix products: 12.3 us -> 0 us
  starting transfers between devices: 10.5 us -> 0 us
  other arithmetic: 5.4 us -> 0 us
    psum x5 -> x0, blocking collectives: 203 us -> none  [the longest x2 118 us: norm_sum(): return lax.psum(jnp.sum(residual * residual, axis=1), 'snp')]
    psum x1 -> x0, waiting for transfers between devices: 134 us -> none  [local(): complete = lax.psum(partial_scores, 'snp')]
    all_gather x1 -> x0, blocking collectives: 57.2 us -> none  [local(): lax.all_gather(rounded, 'ind', axis=0, tiled=True)]
    pallas_call x0 -> x1, Pallas kernels: none -> 52 us  [local(): pl.pallas_call(kernel, out_shape=(jax.ShapeDtypeStruct((TR, COLS), F32),...]
    gather x48 -> x0, local copies, waits for them, and re-layouts: 21 us -> none
    dot_general x3 -> x0, matrix products: 12.3 us -> none  [the longest x2 10.8 us: apply_operator(): jnp.einsum('btk,brk->tbr', windows, blocks, precision=lax.Precision.HIGHEST)]
    ppermute x4 -> x0, starting transfers between devices: 10.5 us -> none  [the longest x2 7.92 us: padded_2(): lax.ppermute(lax.slice_in_dim(block, block.shape[dim] - width, None, axis...]
    unnamed x7 -> x12, local copies, waits for them, and re-layouts: 0.73 us -> 7.06 us
  transfers between devices with their start and end apart: 5 -> 0, of which waited for: 3 -> 0; matrix products, arithmetic and copies ran while one was open for 0% -> 0% of each run, Pallas kernels for 0% -> 0%
where the time goes in v1:
time: 60 us; the launch traced here: 59.8 us
  Pallas kernels  52 us (87%)
  local copies, waits for them, and re-layouts  7.06 us (12%)
  between operations  0.65 us (1%)
    pallas_call x1, Pallas kernels, local(): pl.pallas_call(kernel, out_shape=(jax.ShapeDtypeStruct((TR, COLS), F32),...  52 us
    unnamed x12, local copies, waits for them, and re-layouts  7.06 us

profile of v1, /device:TPU:1, one launch (start us, length us, event | category | flops | bytes accessed | tf_op | source)
XLA Modules:
  0.0 59.8 jit_solution(186604017256239000)
XLA Ops:
  0.6 0.0 copy-start
  0.6 2.2 %copy-done = f32[1024,1024]{1,0:T(8,128)S(1)} copy-done((f32[1024,1024]{1,0:T(8,128)S(1)}, f32[1024,1024]{1,0:T(8,128)}, u32[]{:S(2)}) %copy-start) | copy-done | bytes 4194328
  2.8 0.0 copy-start.1
  2.8 1.6 %copy-done.1 = bf16[1024,1024]{1,0:T(8,128)(2,1)S(1)} copy-done((bf16[1024,1024]{1,0:T(8,128)(2,1)S(1)}, bf16[1024,1024]{1,0:T(8,128)(2,1)}, u32[]{:S(2)}) %copy-start.1) | copy-done | bytes 2097176
  4.4 0.0 copy-start.2
  4.4 0.8 %copy-done.2 = f32[8,1024]{1,0:T(8,128)S(1)} copy-done((f32[8,1024]{1,0:T(8,128)S(1)}, f32[8,1024]{1,0:T(8,128)}, u32[]{:S(2)}) %copy-start.2) | copy-done | bytes 32792
  5.2 0.0 copy-start.3
  5.2 0.7 %copy-done.3 = s32[8]{0:T(128)S(1)} copy-done((s32[8]{0:T(128)S(1)}, s32[8]{0:T(128)}, u32[]{:S(2)}) %copy-start.3) | copy-done | bytes 56
  5.8 0.0 copy-start.4
  5.8 0.7 %copy-done.4 = f32[8]{0:T(128)S(1)} copy-done((f32[8]{0:T(128)S(1)}, f32[8]{0:T(128)}, u32[]{:S(2)}) %copy-start.4) | copy-done | bytes 56
  6.5 52.0 %ldpred_scores.1 = (f32[8,1024]{1,0:T(8,128)S(1)}, f32[32,64]{1,0:T(8,128)S(1)}) custom-call(s32[8]{0:T(128)S(1)} %copy-done.3, f32[8]{0:T(128)S(1)} %copy-done.4, f32[8,1024]{1,0:T(8,128)S(1)} %copy-done.2, f32[1024,1024]{1,0:T(8,128)S(1)} %copy-done, bf16[1024,1024]{1,0:T(8,128)(2,1)S(1)} %copy-done.1), custom_call_target="tpu_custom_call" | custom-call | tf_op jit(solution)/shard_map/ldpred_scores/pallas_call | solution.py:335
  58.5 0.6 %copy.9 = f32[8,1024]{1,0:T(8,128)} copy(f32[8,1024]{1,0:T(8,128)S(1)} %get-tuple-element.8) | data formatting | bytes 65536
  59.2 0.6 %copy.10 = f32[64,32]{0,1:T(8,128)} copy(f32[64,32]{0,1:T(8,128)S(1)} %bitcast.1) | data formatting | bytes 16384
Async XLA Ops:
  0.6 2.2 %copy-start = (f32[1024,1024]{1,0:T(8,128)S(1)}, f32[1024,1024]{1,0:T(8,128)}, u32[]{:S(2)}) copy-start(f32[1024,1024]{1,0:T(8,128)} %ld_ref.1) | copy-start | bytes 12582916
  2.8 1.6 %copy-start.1 = (bf16[1024,1024]{1,0:T(8,128)(2,1)S(1)}, bf16[1024,1024]{1,0:T(8,128)(2,1)}, u32[]{:S(2)}) copy-start(bf16[1024,1024]{1,0:T(8,128)(2,1)} %geno_ref.1) | copy-start | bytes 6291460
  4.4 0.8 %copy-start.2 = (f32[8,1024]{1,0:T(8,128)S(1)}, f32[8,1024]{1,0:T(8,128)}, u32[]{:S(2)}) copy-start(f32[8,1024]{1,0:T(8,128)} %beta_ref.1) | copy-start | bytes 98308
  5.2 0.7 %copy-start.3 = (s32[8]{0:T(128)S(1)}, s32[8]{0:T(128)}, u32[]{:S(2)}) copy-start(s32[8]{0:T(128)} %start_ref.1) | copy-start | bytes 100
  5.8 0.7 %copy-start.4 = (f32[8]{0:T(128)S(1)}, f32[8]{0:T(128)}, u32[]{:S(2)}) copy-start(f32[8]{0:T(128)} %herit_ref.1) | copy-start | bytes 100

commit v2 on v1

--- a/solution.py
+++ b/solution.py
@@ -72,13 +72,16 @@
 
 
 def kernel(
-    start_ref,
-    herit_ref,
-    beta_ref,
+    start_hbm,
+    herit_hbm,
+    beta_hbm,
     ld_ref,
     geno_ref,
     weights_ref,
     scores_ref,
+    start_ref,
+    herit_ref,
+    beta_ref,
     ldbuf,
     hilo,
     geno,
@@ -96,6 +99,7 @@
     stat_in2,
     ld_sem,
     geno_sem,
+    small_sem,
     halo_send,
     halo_recv,
     send_sem,
@@ -113,6 +117,14 @@
     def load(b):
         return pltpu.make_async_copy(ld_ref.at[pl.ds(b * BLK, BLK)], ldbuf.at[b], ld_sem.at[b])
 
+    small = [
+        pltpu.make_async_copy(src, dst, small_sem.at[k])
+        for k, (src, dst) in enumerate(
+            ((beta_hbm, beta_ref), (start_hbm, start_ref), (herit_hbm, herit_ref))
+        )
+    ]
+    for copy in small:
+        copy.start()
     for b in range(NB):
         load(b).start()
     load_geno = pltpu.make_async_copy(geno_ref, geno, geno_sem)
@@ -125,6 +137,8 @@
         pl.semaphore_signal(barrier, inc=1, device_id=(s, ind_peer(dx, dc)), device_id_type=MESH)
     pl.semaphore_wait(barrier, len(SNP_OFFSETS) + len(IND_OFFSETS))
 
+    for copy in small:
+        copy.wait()
     right, left = lax.rem(s + 1, SNP), lax.rem(s + SNP - 1, SNP)
 
     def send_halo(src, turn):
@@ -329,8 +343,7 @@
 
 
 def local(beta_hat, ld_band, band_start, heritability, genotypes):
-    vmem, smem = pl.BlockSpec(memory_space=pltpu.VMEM), pl.BlockSpec(memory_space=pltpu.SMEM)
-    anywhere = pl.BlockSpec(memory_space=pl.ANY)
+    vmem, anywhere = pl.BlockSpec(memory_space=pltpu.VMEM), pl.BlockSpec(memory_space=pl.ANY)
     dma = pltpu.SemaphoreType.DMA
     weights, scores = pl.pallas_call(
         kernel,
@@ -338,9 +351,12 @@
             jax.ShapeDtypeStruct((TR, COLS), F32),
             jax.ShapeDtypeStruct((SHARE, 64), F32),
         ),
-        in_specs=[smem, smem, vmem, anywhere, anywhere],
+        in_specs=[anywhere] * 5,
         out_specs=(vmem, vmem),
         scratch_shapes=[
+            pltpu.SMEM((NB,), jnp.int32),
+            pltpu.SMEM((TR,), F32),
+            pltpu.VMEM((TR, COLS), F32),
             pltpu.VMEM((NB, BLK, COLS), F32),
             pltpu.VMEM((NB, 2 * BLK, SPAN), BF16),
             pltpu.VMEM((1024, COLS), BF16),
@@ -358,6 +374,7 @@
             pltpu.VMEM((IND, 1, BLK), F32),
             dma((NB,)),
             dma,
+            dma((3,)),
             dma((2, 2)),
             dma((2, 2)),
             dma((5,)),
@@ -365,7 +382,7 @@
         ],
         name="ldpred_scores",
         compiler_params=pltpu.CompilerParams(
-            collective_id=0, has_side_effects=True, vmem_limit_bytes=40 << 20
+            collective_id=0, has_side_effects=True, vmem_limit_bytes=60 << 20
         ),
     )(band_start, heritability, beta_hat, ld_band, genotypes)
     return weights, scores.T

time: 60 us -> 55.4 us (0.923)
  local copies, waits for them, and re-layouts: 7.06 us -> 2.7 us
    unnamed x12 -> x2, local copies, waits for them, and re-layouts: 7.06 us -> 2.7 us
where the time goes in v2:
time: 55.4 us; the launch traced here: 55.2 us
  Pallas kernels  51.9 us (94%)
  local copies, waits for them, and re-layouts  2.7 us (5%)
  between operations  0.64 us (1%)
    pallas_call x1, Pallas kernels, local(): pl.pallas_call(kernel, out_shape=(jax.ShapeDtypeStruct((TR, COLS), F32),...  51.9 us
    unnamed x2, local copies, waits for them, and re-layouts  2.7 us

profile of v2, /device:TPU:1, one launch (start us, length us, event | category | flops | bytes accessed | tf_op | source)
XLA Modules:
  0.0 55.2 jit_solution(8043476926308541840)
XLA Ops:
  0.6 51.9 %ldpred_scores.1 = (f32[8,1024]{1,0:T(8,128)}, f32[32,64]{1,0:T(8,128)}) custom-call(s32[8]{0:T(128)} %start_hbm.1, f32[8]{0:T(128)} %herit_hbm.1, f32[8,1024]{1,0:T(8,128)} %beta_hbm.1, f32[1024,1024]{1,0:T(8,128)} %ld_ref.1, bf16[1024,1024]{1,0:T(8,128)(2,1)} %geno_ref.1), custom_call_target="tpu_custom_call" | custom-call | tf_op jit(solution)/shard_map/ldpred_scores/pallas_call | solution.py:348
  52.5 1.4 %copy.9 = f32[8,1024]{1,0:T(8,128)} copy(f32[8,1024]{1,0:T(8,128)} %get-tuple-element.8) | data formatting | bytes 65536
  53.9 1.3 %copy.10 = f32[64,32]{0,1:T(8,128)} copy(f32[64,32]{0,1:T(8,128)} %bitcast.1) | data formatting | bytes 16384

commit v3 on v2

--- a/solution.py
+++ b/solution.py
@@ -77,8 +77,8 @@
     beta_hbm,
     ld_ref,
     geno_ref,
-    weights_ref,
-    scores_ref,
+    weights_out,
+    scores_out,
     start_ref,
     herit_ref,
     beta_ref,
@@ -88,18 +88,21 @@
     acc,
     ubuf,
     halo,
+    basis,
     mom_own,
     mom_in,
-    wall,
+    coef_own,
+    coef_in,
     part,
     part_in,
     stat_own,
     stat_in,
-    stat_own2,
-    stat_in2,
+    weights_ref,
+    scores_ref,
     ld_sem,
     geno_sem,
     small_sem,
+    out_sem,
     halo_send,
     halo_recv,
     send_sem,
@@ -113,6 +116,19 @@
 
     def ind_peer(dx, dc):
         return lax.rem(x + dx, X) * 2 + lax.rem(core + dc, 2)
+
+    near_peers = [
+        (y * Z + lax.rem(z + dz, Z), x * 2 + lax.rem(core + dc, 2))
+        for dz in ring(Z)
+        for dc in (1, 0)
+        if (dz, dc) != (0, 0)
+    ]
+    far_peers = [
+        (lax.rem(y + dy, Y) * Z + z, lax.rem(x + dx, X) * 2 + core)
+        for dx in ring(X)
+        for dy in ring(Y)
+        if (dx, dy) != (0, 0)
+    ]
 
     def load(b):
         return pltpu.make_async_copy(ld_ref.at[pl.ds(b * BLK, BLK)], ldbuf.at[b], ld_sem.at[b])
@@ -165,6 +181,22 @@
         return copies
 
     halo0 = send_halo(beta_ref, 0)
+    beta = beta_ref[...]
+
+    def gather(turn, parts):
+        basis[turn, i] = parts
+        for dx, dc in IND_OFFSETS:
+            pltpu.make_async_remote_copy(
+                src_ref=basis.at[turn, i],
+                dst_ref=basis.at[turn, i],
+                send_sem=send_sem.at[turn],
+                recv_sem=recv_sem.at[turn],
+                device_id=(s, ind_peer(dx, dc)),
+                device_id_type=MESH,
+            ).start()
+
+    beta_parts = split(beta)
+    gather(0, beta_parts)
 
     for b in range(NB):
         load(b).wait()
@@ -182,53 +214,100 @@
 
         lax.fori_loop(0, BLK // 32, rows, 0)
 
-    def off_diagonal(value, turn, copies):
-        parts = split(value)
-        local_part(parts, hilo, acc)
+    def off_diagonal(parts, turn, copies):
         for copy in copies:
             copy.wait_recv()
         halo_part(split(halo[turn, 0]), split(halo[turn, 1]), hilo, acc)
         return acc[...] - (parts[0:8].astype(F32) + parts[8:16].astype(F32))
 
-    beta = beta_ref[...]
-    u = off_diagonal(beta, 0, halo0)
+    local_part(beta_parts, hilo, acc)
+    u = off_diagonal(beta_parts, 0, halo0)
+    u_parts = split(u)
+    gather(1, u_parts)
     ubuf[...] = u
     halo1 = send_halo(ubuf, 1)
 
+    local_part(u_parts, hilo, acc)
     p0 = lane_sum(beta * beta)
     p1 = lane_sum(beta * u)
     theta = jnp.where(p0 > 0, p1 / p0, 0.0)
     e = u - theta * beta
     q = lane_sum(e * e)
     t = lane_sum(e * beta)
-    g = off_diagonal(u, 1, halo1) - theta * u
+
+    slot = {offset: j for j, offset in enumerate(SNP_OFFSETS)}
+    lane = lax.broadcasted_iota(jnp.int32, (1, BLK), 1)
+    half = lane < 64
+
+    def both(value):
+        return value + pltpu.roll(value, 64, value.ndim - 1)
+
+    def partial_scores(turn):
+        wait_for(basis.at[turn, 0 : len(IND_OFFSETS)], recv_sem.at[turn])
+        every = basis[turn].astype(F32)
+        every = jnp.concatenate(
+            [every[:, 0:8].reshape(64, COLS), every[:, 8:16].reshape(64, COLS)], axis=0
+        ).astype(BF16)
+        for dy in ring(Y):
+            group = lax.rem(y + dy, Y)
+            rows = geno[pl.ds(pl.multiple_of(group * 256, 256), 256), :]
+            out = both(lax.dot_general(rows, every, NT, preferred_element_type=F32))
+            out = out.reshape(Z, 2, 16, BLK)
+            part[turn, pl.ds(group * Z, Z)] = jnp.where(half, out[:, 0], out[:, 1])
+            for dz in ring(Z):
+                if (dy, dz) != (0, 0):
+                    peer = group * Z + lax.rem(z + dz, Z)
+                    pltpu.make_async_remote_copy(
+                        src_ref=part.at[turn, peer],
+                        dst_ref=part_in.at[turn, slot[dy, dz]],
+                        send_sem=send_sem.at[2 + turn],
+                        recv_sem=recv_sem.at[2 + turn],
+                        device_id=(peer, i),
+                        device_id_type=MESH,
+                    ).start()
+
+    def total_scores(turn):
+        own = part[turn, s]
+        wait_for(part_in.at[turn], recv_sem.at[2 + turn])
+        return own + jnp.sum(part_in[turn], axis=0)
+
+    load_geno.wait()
+    partial_scores(0)
+
+    g = off_diagonal(u_parts, 1, halo1) - theta * u
     f = lane_sum(e * g)
     h = lane_sum(beta * g)
-
-    lane = lax.broadcasted_iota(jnp.int32, (TR, BLK), 1)
+    tile_lane = lax.broadcasted_iota(jnp.int32, (TR, BLK), 1)
+    tile_row = lax.broadcasted_iota(jnp.int32, (TR, BLK), 0)
     tile = jnp.broadcast_to(p0, (TR, BLK))
     for k, value in enumerate((theta, q, t, f, h)):
-        tile = jnp.where(lane >= 16 * (k + 1), value, tile)
-    mom_own[...] = tile
-    mom_in[len(SNP_OFFSETS)] = tile
+        tile = jnp.where(tile_lane >= 16 * (k + 1), value, tile)
+    tile = jnp.where(tile_lane % 16 == tile_row, tile, 0.0)
+    sums = jnp.sum(tile, axis=0, keepdims=True)
+    mom_own[...] = sums
+    mom_in[len(SNP_OFFSETS)] = sums
     for j, (dy, dz) in enumerate(SNP_OFFSETS):
         pltpu.make_async_remote_copy(
             src_ref=mom_own,
             dst_ref=mom_in.at[j],
-            send_sem=send_sem.at[0],
-            recv_sem=recv_sem.at[0],
+            send_sem=send_sem.at[4],
+            recv_sem=recv_sem.at[4],
             device_id=(snp_peer(dy, dz), i),
             device_id_type=MESH,
         ).start()
 
-    row = lax.broadcasted_iota(jnp.int32, (TR, 1), 0)
-    herit = jnp.zeros((TR, 1), F32)
+    partial_scores(1)
+
+    herit = jnp.ones((1, BLK), F32)
     for k in range(TR):
-        herit = jnp.where(row == k, herit_ref[k], herit)
+        herit = jnp.where(lane == k, herit_ref[k], herit)
     kappa = 1.0 + (M_GENOME / N_GWAS) / herit
 
-    wait_for(mom_in.at[0 : len(SNP_OFFSETS)], recv_sem.at[0])
-    p0_d, th_d, q_d, t_d, f_d, h_d = [mom_in[:, :, 16 * k : 16 * k + 1] for k in range(6)]
+    wait_for(mom_in.at[0 : len(SNP_OFFSETS)], recv_sem.at[4])
+    moments = mom_in[...]
+    p0_d, th_d, q_d, t_d, f_d, h_d = [
+        moments if k == 0 else pltpu.roll(moments, BLK - 16 * k, 2) for k in range(6)
+    ]
     p0 = jnp.sum(p0_d, axis=0)
     theta = jnp.sum(p0_d * th_d + t_d, axis=0) / p0
     delta = th_d - theta[None]
@@ -242,108 +321,96 @@
     a22 = f + kappa * q
     det = a11 * a22 - a12 * a12
     c1 = jnp.where(det > 0, (t * a11 - p0 * a12) / det, 0.0)
-    c0 = (p0 - c1 * a12) / a11
-    weights = (c0 - c1 * theta) * beta + c1 * u
-    weights_ref[...] = weights
-
-    wall[i] = jnp.concatenate([weights[:, 0:HALO], weights[:, HALO:]], axis=0).astype(BF16)
-    for dx, dc in IND_OFFSETS:
+    c0 = (p0 - c1 * a12) / a11 - c1 * theta
+
+    own_lanes = lane < TR
+    coef = jnp.where(own_lanes, c0, 0.0) + pltpu.roll(jnp.where(own_lanes, c1, 0.0), 64, 1)
+    coef = pltpu.roll(coef, i * TR, 1)
+    coef_own[...] = coef
+    coef_in[len(IND_OFFSETS)] = coef
+    for j, (dx, dc) in enumerate(IND_OFFSETS):
         pltpu.make_async_remote_copy(
-            src_ref=wall.at[i],
-            dst_ref=wall.at[i],
-            send_sem=send_sem.at[1],
-            recv_sem=recv_sem.at[1],
+            src_ref=coef_own,
+            dst_ref=coef_in.at[j],
+            send_sem=send_sem.at[5],
+            recv_sem=recv_sem.at[5],
             device_id=(s, ind_peer(dx, dc)),
             device_id_type=MESH,
         ).start()
-    load_geno.wait()
-    wait_for(wall.at[0 : len(IND_OFFSETS)], recv_sem.at[1])
-    every = wall[...].astype(F32)
-    rounded = jnp.concatenate(
-        [every[:, 0:8].reshape(64, HALO), every[:, 8:16].reshape(64, HALO)], axis=1
-    ).astype(BF16)
-
-    slot = {offset: j for j, offset in enumerate(SNP_OFFSETS)}
-    for dy in ring(Y):
-        group = lax.rem(y + dy, Y)
-        rows = geno[pl.ds(pl.multiple_of(group * 256, 256), 256), :]
-        out = lax.dot_general(rows, rounded, NT, preferred_element_type=F32).reshape(Z, 2, 16, 64)
-        part[pl.ds(group * Z, Z)] = jnp.concatenate([out[:, 0], out[:, 1]], axis=2)
-        for dz in ring(Z):
-            if (dy, dz) != (0, 0):
-                peer = group * Z + lax.rem(z + dz, Z)
-                pltpu.make_async_remote_copy(
-                    src_ref=part.at[peer],
-                    dst_ref=part_in.at[slot[dy, dz]],
-                    send_sem=send_sem.at[2],
-                    recv_sem=recv_sem.at[2],
-                    device_id=(peer, i),
-                    device_id_type=MESH,
-                ).start()
-    own = part[s]
-    wait_for(part_in, recv_sem.at[2])
-    raw = own + jnp.sum(part_in[...], axis=0)
-
-    half = lax.broadcasted_iota(jnp.int32, (1, BLK), 1) < 64
-
-    def both(value):
-        return value + pltpu.roll(value, 64, 1)
+
+    diagonal = tile_lane == tile_row
+    c0 = lane_sum(jnp.where(diagonal, c0, 0.0))
+    c1 = lane_sum(jnp.where(diagonal, c1, 0.0))
+    weights_ref[...] = c0 * beta + c1 * u
+    store_weights = pltpu.make_async_copy(weights_ref, weights_out, out_sem.at[0])
+    store_weights.start()
+
+    beta_scores = total_scores(0)
+    wait_for(coef_in.at[0 : len(IND_OFFSETS)], recv_sem.at[5])
+    coef = jnp.sum(coef_in[...], axis=0)
+    swapped = pltpu.roll(coef, 64, 1)
+    beta_scores = beta_scores * jnp.where(half, coef, swapped)
+    raw = beta_scores + total_scores(1) * jnp.where(half, swapped, coef)
 
     mean = both(jnp.sum(raw, axis=0, keepdims=True)) * (1.0 / SHARE)
     spread = both(jnp.sum((raw - mean) * (raw - mean), axis=0, keepdims=True))
     stat = jnp.where(half, mean, spread)
-
-    def merge(values, count, size):
+    size = SHARE
+    for turn, peers in enumerate((near_peers, far_peers)):
+        stat_own[turn] = stat
+        stat_in[turn, len(peers)] = stat
+        for j, peer in enumerate(peers):
+            pltpu.make_async_remote_copy(
+                src_ref=stat_own.at[turn],
+                dst_ref=stat_in.at[turn, j],
+                send_sem=send_sem.at[6 + turn],
+                recv_sem=recv_sem.at[6 + turn],
+                device_id=peer,
+                device_id_type=MESH,
+            ).start()
+        wait_for(stat_in.at[turn, 0 : len(peers)], recv_sem.at[6 + turn])
+        count = len(peers) + 1
+        values = stat_in[turn]
         total = jnp.sum(values, axis=0)
         mean = total * (1.0 / count)
         apart = jnp.where(half, values - mean, 0.0)
         squares = jnp.sum(apart * apart, axis=0) * float(size)
-        return jnp.where(half, mean, total + pltpu.roll(squares, 64, 1))
-
-    stat_own[...] = stat
-    stat_in[len(SNP_OFFSETS)] = stat
-    for j, (dy, dz) in enumerate(SNP_OFFSETS):
-        pltpu.make_async_remote_copy(
-            src_ref=stat_own,
-            dst_ref=stat_in.at[j],
-            send_sem=send_sem.at[3],
-            recv_sem=recv_sem.at[3],
-            device_id=(snp_peer(dy, dz), i),
-            device_id_type=MESH,
-        ).start()
-    wait_for(stat_in.at[0 : len(SNP_OFFSETS)], recv_sem.at[3])
-    stat = merge(stat_in[...], SNP, SHARE)
-    stat_own2[...] = stat
-    stat_in2[len(IND_OFFSETS)] = stat
-    for j, (dx, dc) in enumerate(IND_OFFSETS):
-        pltpu.make_async_remote_copy(
-            src_ref=stat_own2,
-            dst_ref=stat_in2.at[j],
-            send_sem=send_sem.at[4],
-            recv_sem=recv_sem.at[4],
-            device_id=(s, ind_peer(dx, dc)),
-            device_id_type=MESH,
-        ).start()
-    wait_for(stat_in2.at[0 : len(IND_OFFSETS)], recv_sem.at[4])
-    stat = merge(stat_in2[...], IND, SHARE * SNP)
+        stat = jnp.where(half, mean, total + pltpu.roll(squares, 64, 1))
+        size *= count
     swapped = pltpu.roll(stat, 64, 1)
     mean = jnp.where(half, stat, swapped)
-    variance = jnp.where(half, swapped, stat) * (1.0 / (SHARE * SNP * IND))
+    variance = jnp.where(half, swapped, stat) * (1.0 / size)
     scores = (raw - mean) * lax.rsqrt(variance + 1e-05)
     scores_ref[0:16, :] = scores[:, 0:64]
     scores_ref[16:32, :] = scores[:, 64:128]
+    store_scores = pltpu.make_async_copy(scores_ref, scores_out, out_sem.at[1])
+    store_scores.start()
 
     for copy in halo0 + halo1:
         copy.wait_send()
-    wait_for(mom_in.at[0 : len(SNP_OFFSETS)], send_sem.at[0])
-    wait_for(wall.at[0 : len(IND_OFFSETS)], send_sem.at[1])
-    wait_for(part_in, send_sem.at[2])
-    wait_for(stat_in.at[0 : len(SNP_OFFSETS)], send_sem.at[3])
-    wait_for(stat_in2.at[0 : len(IND_OFFSETS)], send_sem.at[4])
+    for turn in range(2):
+        wait_for(basis.at[turn, 0 : len(IND_OFFSETS)], send_sem.at[turn])
+        wait_for(part_in.at[turn], send_sem.at[2 + turn])
+        wait_for(stat_in.at[turn, 0:15], send_sem.at[6 + turn])
+    wait_for(mom_in.at[0 : len(SNP_OFFSETS)], send_sem.at[4])
+    wait_for(coef_in.at[0 : len(IND_OFFSETS)], send_sem.at[5])
+    store_weights.wait()
+    store_scores.wait()
+
+
+def hand_over(weights_ref, scores_ref, weights_out, scores_out, sem):
+    copies = [
+        pltpu.make_async_copy(weights_ref, weights_out, sem.at[0]),
+        pltpu.make_async_copy(scores_ref, scores_out, sem.at[1]),
+    ]
+    for copy in copies:
+        copy.start()
+    for copy in copies:
+        copy.wait()
 
 
 def local(beta_hat, ld_band, band_start, heritability, genotypes):
-    vmem, anywhere = pl.BlockSpec(memory_space=pltpu.VMEM), pl.BlockSpec(memory_space=pl.ANY)
+    anywhere = pl.BlockSpec(memory_space=pl.ANY)
     dma = pltpu.SemaphoreType.DMA
     weights, scores = pl.pallas_call(
         kernel,
@@ -352,7 +419,7 @@
             jax.ShapeDtypeStruct((SHARE, 64), F32),
         ),
         in_specs=[anywhere] * 5,
-        out_specs=(vmem, vmem),
+        out_specs=(anywhere, anywhere),
         scratch_shapes=[
             pltpu.SMEM((NB,), jnp.int32),
             pltpu.SMEM((TR,), F32),
@@ -363,28 +430,43 @@
             pltpu.VMEM((TR, COLS), F32),
             pltpu.VMEM((TR, COLS), F32),
             pltpu.VMEM((2, 2, TR, HALO), F32),
-            pltpu.VMEM((TR, BLK), F32),
-            pltpu.VMEM((SNP, TR, BLK), F32),
-            pltpu.VMEM((IND, 16, HALO), BF16),
-            pltpu.VMEM((SNP, 16, BLK), F32),
-            pltpu.VMEM((SNP - 1, 16, BLK), F32),
+            pltpu.VMEM((2, IND, 16, COLS), BF16),
             pltpu.VMEM((1, BLK), F32),
             pltpu.VMEM((SNP, 1, BLK), F32),
             pltpu.VMEM((1, BLK), F32),
             pltpu.VMEM((IND, 1, BLK), F32),
+            pltpu.VMEM((2, SNP, 16, BLK), F32),
+            pltpu.VMEM((2, SNP - 1, 16, BLK), F32),
+            pltpu.VMEM((2, 1, BLK), F32),
+            pltpu.VMEM((2, 16, 1, BLK), F32),
+            pltpu.VMEM((TR, COLS), F32),
+            pltpu.VMEM((SHARE, 64), F32),
             dma((NB,)),
             dma,
             dma((3,)),
+            dma((2,)),
             dma((2, 2)),
             dma((2, 2)),
-            dma((5,)),
-            dma((5,)),
+            dma((8,)),
+            dma((8,)),
         ],
         name="ldpred_scores",
         compiler_params=pltpu.CompilerParams(
             collective_id=0, has_side_effects=True, vmem_limit_bytes=60 << 20
         ),
     )(band_start, heritability, beta_hat, ld_band, genotypes)
+    weights, scores = pl.pallas_call(
+        hand_over,
+        out_shape=(
+            jax.ShapeDtypeStruct((TR, COLS), F32),
+            jax.ShapeDtypeStruct((SHARE, 64), F32),
+        ),
+        in_specs=[anywhere] * 2,
+        out_specs=(anywhere, anywhere),
+        scratch_shapes=[dma((2,))],
+        name="hand_over",
+        compiler_params=pltpu.CompilerParams(vmem_limit_bytes=60 << 20),
+    )(weights, scores)
     return weights, scores.T
 
 

time: 55.4 us -> 47.2 us (0.85)
  Pallas kernels: 51.9 us -> 46.5 us
  local copies, waits for them, and re-layouts: 2.7 us -> 0 us
    pallas_call x1, Pallas kernels: 51.9 us -> 43.9 us  [local(): pl.pallas_call(kernel, out_shape=(jax.ShapeDtypeStruct((TR, COLS), F32),...]
    unnamed x2 -> x0, local copies, waits for them, and re-layouts: 2.7 us -> none
    pallas_call x0 -> x1, Pallas kernels: none -> 2.61 us  [local(): pl.pallas_call(hand_over, out_shape=(jax.ShapeDtypeStruct((TR, COLS), F32...]
where the time goes in v3:
time: 47.2 us; the launch traced here: 47.1 us
  Pallas kernels  46.5 us (99%)
  between operations  0.64 us (1%)
    pallas_call x1, Pallas kernels, local(): pl.pallas_call(kernel, out_shape=(jax.ShapeDtypeStruct((TR, COLS), F32),...  43.9 us
    pallas_call x1, Pallas kernels, local(): pl.pallas_call(hand_over, out_shape=(jax.ShapeDtypeStruct((TR, COLS), F32...  2.61 us

profile of v3, /device:TPU:1, one launch (start us, length us, event | category | flops | bytes accessed | tf_op | source)
XLA Modules:
  0.0 47.1 jit_solution(17067267021284864815)
XLA Ops:
  0.6 43.9 %ldpred_scores.1 = (f32[8,1024]{1,0:T(8,128)}, f32[32,64]{1,0:T(8,128)}) custom-call(s32[8]{0:T(128)} %start_hbm.1, f32[8]{0:T(128)} %herit_hbm.1, f32[8,1024]{1,0:T(8,128)} %beta_hbm.1, f32[1024,1024]{1,0:T(8,128)} %ld_ref.1, bf16[1024,1024]{1,0:T(8,128)(2,1)} %geno_ref.1), custom_call_target="tpu_custom_call" | custom-call | tf_op jit(solution)/shard_map/ldpred_scores/pallas_call | solution.py:415
  44.5 2.6 %hand_over.1 = (f32[8,1024]{1,0:T(8,128)}, f32[32,64]{1,0:T(8,128)}) custom-call(f32[8,1024]{1,0:T(8,128)} %get-tuple-element.6.weights_ref, f32[32,64]{1,0:T(8,128)} %get-tuple-element.7.scores_ref), custom_call_target="tpu_custom_call" | custom-call | tf_op jit(solution)/shard_map/hand_over/pallas_call | solution.py:458

commit v4 on v3

--- a/solution.py
+++ b/solution.py
@@ -30,6 +30,10 @@
 SNP_OFFSETS = sorted(
     ((a, b) for a in range(Y) for b in range(Z) if (a, b) != (0, 0)),
     key=lambda q: -(min(q[0], Y - q[0]) + min(q[1], Z - q[1])),
+)
+CHIP_OFFSETS = sorted(
+    ((a, b, c) for a in range(X) for b in range(Y) for c in range(Z) if (a, b, c) != (0, 0, 0)),
+    key=lambda q: -(min(q[0], X - q[0]) + min(q[1], Y - q[1]) + min(q[2], Z - q[2])),
 )
 IND_OFFSETS = [(a, c) for a in ring(X) for c in (1, 0) if (a, c) != (0, 0)]
 
@@ -95,6 +99,9 @@
     coef_in,
     part,
     part_in,
+    lines_in,
+    line_own,
+    line_in,
     stat_own,
     stat_in,
     weights_ref,
@@ -117,17 +124,10 @@
     def ind_peer(dx, dc):
         return lax.rem(x + dx, X) * 2 + lax.rem(core + dc, 2)
 
-    near_peers = [
-        (y * Z + lax.rem(z + dz, Z), x * 2 + lax.rem(core + dc, 2))
-        for dz in ring(Z)
-        for dc in (1, 0)
-        if (dz, dc) != (0, 0)
-    ]
+    near_peers = [(s, i + 1 - 2 * core)]
     far_peers = [
-        (lax.rem(y + dy, Y) * Z + z, lax.rem(x + dx, X) * 2 + core)
-        for dx in ring(X)
-        for dy in ring(Y)
-        if (dx, dy) != (0, 0)
+        (lax.rem(y + dy, Y) * Z + lax.rem(z + dz, Z), lax.rem(x + dx, X) * 2 + core)
+        for dx, dy, dz in CHIP_OFFSETS
     ]
 
     def load(b):
@@ -178,8 +178,10 @@
         ]
         for copy in copies:
             copy.start()
+            pending.append(copy.wait_send)
         return copies
 
+    pending = []
     halo0 = send_halo(beta_ref, 0)
     beta = beta_ref[...]
 
@@ -194,6 +196,7 @@
                 device_id=(s, ind_peer(dx, dc)),
                 device_id_type=MESH,
             ).start()
+        pending.append(lambda: wait_for(basis.at[turn, 0 : len(IND_OFFSETS)], send_sem.at[turn]))
 
     beta_parts = split(beta)
     gather(0, beta_parts)
@@ -254,22 +257,57 @@
             out = both(lax.dot_general(rows, every, NT, preferred_element_type=F32))
             out = out.reshape(Z, 2, 16, BLK)
             part[turn, pl.ds(group * Z, Z)] = jnp.where(half, out[:, 0], out[:, 1])
+            if turn == 0:
+                if dy:
+                    along_y(dy)
+                continue
             for dz in ring(Z):
                 if (dy, dz) != (0, 0):
                     peer = group * Z + lax.rem(z + dz, Z)
                     pltpu.make_async_remote_copy(
                         src_ref=part.at[turn, peer],
-                        dst_ref=part_in.at[turn, slot[dy, dz]],
-                        send_sem=send_sem.at[2 + turn],
-                        recv_sem=recv_sem.at[2 + turn],
+                        dst_ref=part_in.at[slot[dy, dz]],
+                        send_sem=send_sem.at[3],
+                        recv_sem=recv_sem.at[3],
                         device_id=(peer, i),
                         device_id_type=MESH,
                     ).start()
+        if turn == 1:
+            pending.append(lambda: wait_for(part_in, send_sem.at[3]))
+
+    def along_y(dy):
+        group = lax.rem(y + dy, Y)
+        pltpu.make_async_remote_copy(
+            src_ref=part.at[0, pl.ds(group * Z, Z)],
+            dst_ref=lines_in.at[dy - 1],
+            send_sem=send_sem.at[2],
+            recv_sem=recv_sem.at[2],
+            device_id=(group * Z + z, i),
+            device_id_type=MESH,
+        ).start()
+
+    def along_z():
+        wait_for(lines_in, recv_sem.at[2])
+        line_own[...] = part[0, pl.ds(y * Z, Z)] + jnp.sum(lines_in[...], axis=0)
+        for dz in ring(Z)[:-1]:
+            peer = lax.rem(z + dz, Z)
+            pltpu.make_async_remote_copy(
+                src_ref=line_own.at[peer],
+                dst_ref=line_in.at[dz - 1],
+                send_sem=send_sem.at[8],
+                recv_sem=recv_sem.at[8],
+                device_id=(y * Z + peer, i),
+                device_id_type=MESH,
+            ).start()
+        pending.append(lambda: wait_for(lines_in, send_sem.at[2]))
+        pending.append(lambda: wait_for(line_in, send_sem.at[8]))
 
     def total_scores(turn):
-        own = part[turn, s]
-        wait_for(part_in.at[turn], recv_sem.at[2 + turn])
-        return own + jnp.sum(part_in[turn], axis=0)
+        if turn == 0:
+            wait_for(line_in, recv_sem.at[8])
+            return line_own[z] + jnp.sum(line_in[...], axis=0)
+        wait_for(part_in, recv_sem.at[3])
+        return part[1, s] + jnp.sum(part_in[...], axis=0)
 
     load_geno.wait()
     partial_scores(0)
@@ -296,7 +334,10 @@
             device_id_type=MESH,
         ).start()
 
+    pending.append(lambda: wait_for(mom_in.at[0 : len(SNP_OFFSETS)], send_sem.at[4]))
+
     partial_scores(1)
+    along_z()
 
     herit = jnp.ones((1, BLK), F32)
     for k in range(TR):
@@ -338,6 +379,8 @@
             device_id_type=MESH,
         ).start()
 
+    pending.append(lambda: wait_for(coef_in.at[0 : len(IND_OFFSETS)], send_sem.at[5]))
+
     diagonal = tile_lane == tile_row
     c0 = lane_sum(jnp.where(diagonal, c0, 0.0))
     c1 = lane_sum(jnp.where(diagonal, c1, 0.0))
@@ -357,6 +400,7 @@
     stat = jnp.where(half, mean, spread)
     size = SHARE
     for turn, peers in enumerate((near_peers, far_peers)):
+        count = len(peers) + 1
         stat_own[turn] = stat
         stat_in[turn, len(peers)] = stat
         for j, peer in enumerate(peers):
@@ -368,9 +412,10 @@
                 device_id=peer,
                 device_id_type=MESH,
             ).start()
-        wait_for(stat_in.at[turn, 0 : len(peers)], recv_sem.at[6 + turn])
-        count = len(peers) + 1
-        values = stat_in[turn]
+        arrived = stat_in.at[turn, 0 : len(peers)]
+        pending.append(lambda turn=turn, arrived=arrived: wait_for(arrived, send_sem.at[6 + turn]))
+        wait_for(arrived, recv_sem.at[6 + turn])
+        values = stat_in[turn, 0:count]
         total = jnp.sum(values, axis=0)
         mean = total * (1.0 / count)
         apart = jnp.where(half, values - mean, 0.0)
@@ -386,31 +431,19 @@
     store_scores = pltpu.make_async_copy(scores_ref, scores_out, out_sem.at[1])
     store_scores.start()
 
-    for copy in halo0 + halo1:
-        copy.wait_send()
-    for turn in range(2):
-        wait_for(basis.at[turn, 0 : len(IND_OFFSETS)], send_sem.at[turn])
-        wait_for(part_in.at[turn], send_sem.at[2 + turn])
-        wait_for(stat_in.at[turn, 0:15], send_sem.at[6 + turn])
-    wait_for(mom_in.at[0 : len(SNP_OFFSETS)], send_sem.at[4])
-    wait_for(coef_in.at[0 : len(IND_OFFSETS)], send_sem.at[5])
+    for drain in pending:
+        drain()
     store_weights.wait()
     store_scores.wait()
 
 
-def hand_over(weights_ref, scores_ref, weights_out, scores_out, sem):
-    copies = [
-        pltpu.make_async_copy(weights_ref, weights_out, sem.at[0]),
-        pltpu.make_async_copy(scores_ref, scores_out, sem.at[1]),
-    ]
-    for copy in copies:
-        copy.start()
-    for copy in copies:
-        copy.wait()
+def hand_over(weights_ref, scores_ref, weights_out, scores_out):
+    weights_out[...] = weights_ref[...]
+    scores_out[...] = scores_ref[...]
 
 
 def local(beta_hat, ld_band, band_start, heritability, genotypes):
-    anywhere = pl.BlockSpec(memory_space=pl.ANY)
+    vmem, anywhere = pl.BlockSpec(memory_space=pltpu.VMEM), pl.BlockSpec(memory_space=pl.ANY)
     dma = pltpu.SemaphoreType.DMA
     weights, scores = pl.pallas_call(
         kernel,
@@ -436,9 +469,12 @@
             pltpu.VMEM((1, BLK), F32),
             pltpu.VMEM((IND, 1, BLK), F32),
             pltpu.VMEM((2, SNP, 16, BLK), F32),
-            pltpu.VMEM((2, SNP - 1, 16, BLK), F32),
+            pltpu.VMEM((SNP - 1, 16, BLK), F32),
+            pltpu.VMEM((Y - 1, Z, 16, BLK), F32),
+            pltpu.VMEM((Z, 16, BLK), F32),
+            pltpu.VMEM((Z - 1, 16, BLK), F32),
             pltpu.VMEM((2, 1, BLK), F32),
-            pltpu.VMEM((2, 16, 1, BLK), F32),
+            pltpu.VMEM((2, X * Y * Z, 1, BLK), F32),
             pltpu.VMEM((TR, COLS), F32),
             pltpu.VMEM((SHARE, 64), F32),
             dma((NB,)),
@@ -447,8 +483,8 @@
             dma((2,)),
             dma((2, 2)),
             dma((2, 2)),
-            dma((8,)),
-            dma((8,)),
+            dma((9,)),
+            dma((9,)),
         ],
         name="ldpred_scores",
         compiler_params=pltpu.CompilerParams(
@@ -461,9 +497,8 @@
             jax.ShapeDtypeStruct((TR, COLS), F32),
             jax.ShapeDtypeStruct((SHARE, 64), F32),
         ),
-        in_specs=[anywhere] * 2,
-        out_specs=(anywhere, anywhere),
-        scratch_shapes=[dma((2,))],
+        in_specs=[vmem] * 2,
+        out_specs=(vmem, vmem),
         name="hand_over",
         compiler_params=pltpu.CompilerParams(vmem_limit_bytes=60 << 20),
     )(weights, scores)

time: 47.2 us -> 43.6 us (0.924)
  Pallas kernels: 46.5 us -> 42.8 us
    pallas_call x1, Pallas kernels: 43.9 us -> 41.5 us  [local(): pl.pallas_call(kernel, out_shape=(jax.ShapeDtypeStruct((TR, COLS), F32),...]
    pallas_call x1, Pallas kernels: 2.61 us -> 1.38 us  [local(): pl.pallas_call(hand_over, out_shape=(jax.ShapeDtypeStruct((TR, COLS), F32...]
where the time goes in v4:
time: 43.6 us; the launch traced here: 43.5 us
  Pallas kernels  42.8 us (98%)
  between operations  0.64 us (1%)
    pallas_call x1, Pallas kernels, local(): pl.pallas_call(kernel, out_shape=(jax.ShapeDtypeStruct((TR, COLS), F32),...  41.5 us
    pallas_call x1, Pallas kernels, local(): pl.pallas_call(hand_over, out_shape=(jax.ShapeDtypeStruct((TR, COLS), F32...  1.38 us

profile of v4, /device:TPU:1, one launch (start us, length us, event | category | flops | bytes accessed | tf_op | source)
XLA Modules:
  0.0 43.5 jit_solution(12597377514707506084)
XLA Ops:
  0.6 41.5 %ldpred_scores.1 = (f32[8,1024]{1,0:T(8,128)}, f32[32,64]{1,0:T(8,128)}) custom-call(s32[8]{0:T(128)} %start_hbm.1, f32[8]{0:T(128)} %herit_hbm.1, f32[8,1024]{1,0:T(8,128)} %beta_hbm.1, f32[1024,1024]{1,0:T(8,128)} %ld_ref.1, bf16[1024,1024]{1,0:T(8,128)(2,1)} %geno_ref.1), custom_call_target="tpu_custom_call" | custom-call | tf_op jit(solution)/shard_map/ldpred_scores/pallas_call | solution.py:448
  42.1 1.4 %hand_over.1 = (f32[8,1024]{1,0:T(8,128)}, f32[32,64]{1,0:T(8,128)}) custom-call(f32[8,1024]{1,0:T(8,128)} %get-tuple-element.6.weights_ref, f32[32,64]{1,0:T(8,128)} %get-tuple-element.7.scores_ref), custom_call_target="tpu_custom_call" | custom-call | tf_op jit(solution)/shard_map/hand_over/pallas_call | solution.py:494

commit v5 on v4

--- a/solution.py
+++ b/solution.py
@@ -16,7 +16,6 @@
 TR = 8
 COLS = NB * BLK
 HALO = 512
-SPAN = 1152
 SHARE = 32
 MESH = pl.DeviceIdType.MESH
 NT = (((1,), (1,)), ((), ()))
@@ -47,24 +46,39 @@
     return out[0:8, 0:BLK] + out[8:16, 0:BLK] + out[0:8, BLK:] + out[8:16, BLK:]
 
 
-def local_part(vec, hilo, acc):
+def window(padded, first, width, shift):
+    segment = padded[:, first : first + width + BLK]
+    return split(pltpu.roll(segment, width + BLK - shift, 1)[:, :width])
+
+
+def product(b, vec, k0, hilo):
+    out = lax.dot_general(
+        vec, hilo[b, :, k0 : k0 + vec.shape[1]], NT, preferred_element_type=F32
+    )
+    return fold(out)
+
+
+def local_part(value, shifts, hilo, acc):
+    empty = jnp.zeros((TR, HALO), F32)
+    padded = jnp.concatenate([empty, value, empty], axis=1)
     for b in range(NB):
-        own0, own1 = max(0, BLK * b - HALO), min(COLS, BLK * b + SPAN - HALO)
-        k0 = own0 + HALO - BLK * b
-        out = lax.dot_general(
-            vec[:, own0:own1], hilo[b, :, k0 : k0 + own1 - own0], NT, preferred_element_type=F32
-        )
-        acc[:, b * BLK : (b + 1) * BLK] = fold(out)
-
-
-def halo_part(left, right, hilo, acc):
+        k0, k1 = max(0, 384 - BLK * b), min(COLS, 1536 - BLK * b)
+        vec = window(padded, BLK * b + k0, k1 - k0, shifts[b])
+        acc[:, b * BLK : (b + 1) * BLK] = product(b, vec, k0, hilo)
+
+
+def halo_part(left, right, shifts, hilo, acc):
+    empty = jnp.zeros((TR, BLK), F32)
+    left = jnp.concatenate([left, empty], axis=1)
+    right = jnp.concatenate([empty, right], axis=1)
     for b in range(NB):
         if b < 4:
-            vec, k0, k1 = left[:, BLK * b :], 0, HALO - BLK * b
+            k0 = 0
+            vec = window(left, BLK * b, HALO - BLK * b, shifts[b])
         else:
-            vec, k0, k1 = right[:, : BLK * (b - 3)], HALO + COLS - BLK * b, SPAN
-        out = lax.dot_general(vec, hilo[b, :, k0:k1], NT, preferred_element_type=F32)
-        acc[:, b * BLK : (b + 1) * BLK] += fold(out)
+            k0 = 1408 - BLK * b
+            vec = window(right, 0, COLS - k0, shifts[b])
+        acc[:, b * BLK : (b + 1) * BLK] += product(b, vec, k0, hilo)
 
 
 def wait_for(ref, sem):
@@ -201,15 +215,13 @@
     beta_parts = split(beta)
     gather(0, beta_parts)
 
+    shifts = [start_ref[b] - (BLK * (s * NB + b) - HALO) for b in range(NB)]
     for b in range(NB):
         load(b).wait()
-        shift = start_ref[b] - (BLK * (s * NB + b) - HALO)
-
-        def rows(k, carry, b=b, shift=shift):
+
+        def rows(k, carry, b=b):
             r0 = pl.multiple_of(k * 32, 32)
             value = ldbuf[b, pl.ds(r0, 32), :]
-            value = jnp.concatenate([value, jnp.zeros((32, SPAN - COLS), F32)], axis=1)
-            value = pltpu.roll(value, shift, 1)
             high = value.astype(BF16)
             hilo[b, pl.ds(r0, 32), :] = high
             hilo[b, pl.ds(BLK + r0, 32), :] = (value - high.astype(F32)).astype(BF16)
@@ -220,17 +232,17 @@
     def off_diagonal(parts, turn, copies):
         for copy in copies:
             copy.wait_recv()
-        halo_part(split(halo[turn, 0]), split(halo[turn, 1]), hilo, acc)
+        halo_part(halo[turn, 0], halo[turn, 1], shifts, hilo, acc)
         return acc[...] - (parts[0:8].astype(F32) + parts[8:16].astype(F32))
 
-    local_part(beta_parts, hilo, acc)
+    local_part(beta, shifts, hilo, acc)
     u = off_diagonal(beta_parts, 0, halo0)
     u_parts = split(u)
     gather(1, u_parts)
     ubuf[...] = u
     halo1 = send_halo(ubuf, 1)
 
-    local_part(u_parts, hilo, acc)
+    local_part(u, shifts, hilo, acc)
     p0 = lane_sum(beta * beta)
     p1 = lane_sum(beta * u)
     theta = jnp.where(p0 > 0, p1 / p0, 0.0)
@@ -458,7 +470,7 @@
             pltpu.SMEM((TR,), F32),
             pltpu.VMEM((TR, COLS), F32),
             pltpu.VMEM((NB, BLK, COLS), F32),
-            pltpu.VMEM((NB, 2 * BLK, SPAN), BF16),
+            pltpu.VMEM((NB, 2 * BLK, COLS), BF16),
             pltpu.VMEM((1024, COLS), BF16),
             pltpu.VMEM((TR, COLS), F32),
             pltpu.VMEM((TR, COLS), F32),

time: 43.6 us -> 42.3 us (0.970)
  Pallas kernels: 42.8 us -> 41.5 us
    pallas_call x1, Pallas kernels: 41.5 us -> 40.1 us  [local(): pl.pallas_call(kernel, out_shape=(jax.ShapeDtypeStruct((TR, COLS), F32),...]
where the time goes in v5:
time: 42.3 us; the launch traced here: 42.1 us
  Pallas kernels  41.5 us (98%)
  between operations  0.64 us (2%)
    pallas_call x1, Pallas kernels, local(): pl.pallas_call(kernel, out_shape=(jax.ShapeDtypeStruct((TR, COLS), F32),...  40.1 us
    pallas_call x1, Pallas kernels, local(): pl.pallas_call(hand_over, out_shape=(jax.ShapeDtypeStruct((TR, COLS), F32...  1.38 us

profile of v5, /device:TPU:1, one launch (start us, length us, event | category | flops | bytes accessed | tf_op | source)
XLA Modules:
  0.0 42.1 jit_solution(8183017911088654805)
XLA Ops:
  0.6 40.1 %ldpred_scores.1 = (f32[8,1024]{1,0:T(8,128)}, f32[32,64]{1,0:T(8,128)}) custom-call(s32[8]{0:T(128)} %start_hbm.1, f32[8]{0:T(128)} %herit_hbm.1, f32[8,1024]{1,0:T(8,128)} %beta_hbm.1, f32[1024,1024]{1,0:T(8,128)} %ld_ref.1, bf16[1024,1024]{1,0:T(8,128)(2,1)} %geno_ref.1), custom_call_target="tpu_custom_call" | custom-call | tf_op jit(solution)/shard_map/ldpred_scores/pallas_call | solution.py:460
  40.7 1.4 %hand_over.1 = (f32[8,1024]{1,0:T(8,128)}, f32[32,64]{1,0:T(8,128)}) custom-call(f32[8,1024]{1,0:T(8,128)} %get-tuple-element.6.weights_ref, f32[32,64]{1,0:T(8,128)} %get-tuple-element.7.scores_ref), custom_call_target="tpu_custom_call" | custom-call | tf_op jit(solution)/shard_map/hand_over/pallas_call | solution.py:506

commit v6 on v5

--- a/solution.py
+++ b/solution.py
@@ -128,6 +128,7 @@
     halo_recv,
     send_sem,
     recv_sem,
+    word,
 ):
     s, i = lax.axis_index("snp"), lax.axis_index("ind")
     y, z, x, core = s // Z, s % Z, i // 2, i % 2
@@ -161,16 +162,45 @@
     load_geno.start()
 
     barrier = pltpu.get_barrier_semaphore()
-    for dy, dz in SNP_OFFSETS:
-        pl.semaphore_signal(barrier, inc=1, device_id=(snp_peer(dy, dz), i), device_id_type=MESH)
-    for dx, dc in IND_OFFSETS:
-        pl.semaphore_signal(barrier, inc=1, device_id=(s, ind_peer(dx, dc)), device_id_type=MESH)
-    pl.semaphore_wait(barrier, len(SNP_OFFSETS) + len(IND_OFFSETS))
+    right, left = lax.rem(s + 1, SNP), lax.rem(s + SNP - 1, SNP)
+    around_z = [(snp_peer(0, 1), i), (snp_peer(0, Z - 1), i)]
+    around_y = [(snp_peer(dy, 0), i) for dy in range(1, Y)]
+    beside = [(s, ind_peer(dx, dc)) for dx, dc in IND_OFFSETS]
+
+    def signal(sem, peer):
+        pl.semaphore_signal(sem, inc=1, device_id=peer, device_id_type=MESH)
+
+    for peer in around_z + around_y + beside:
+        signal(barrier, peer)
+
+    @pl.when(z == Z - 1)
+    def _():
+        signal(barrier, (right, i))
+
+    @pl.when(z == 0)
+    def _():
+        signal(barrier, (left, i))
+
+    ends = jnp.where(lax.rem(z + 1, Z) < 2, 1, 0)
+    pl.semaphore_wait(barrier, len(around_z + around_y + beside) + ends)
+
+    steps = [
+        around_z,
+        [(snp_peer(0, 2), i), (snp_peer(0, Z - 2), i)],
+        around_y,
+    ]
+
+    def tell(step):
+        for peer in steps[step]:
+            signal(word.at[step], peer)
+
+    def hear(step):
+        pl.semaphore_wait(word.at[step], len(steps[step]))
+
+    tell(0)
 
     for copy in small:
         copy.wait()
-    right, left = lax.rem(s + 1, SNP), lax.rem(s + SNP - 1, SNP)
-
     def send_halo(src, turn):
         copies = [
             pltpu.make_async_remote_copy(
@@ -236,19 +266,15 @@
         return acc[...] - (parts[0:8].astype(F32) + parts[8:16].astype(F32))
 
     local_part(beta, shifts, hilo, acc)
+    hear(0)
+    tell(1)
     u = off_diagonal(beta_parts, 0, halo0)
     u_parts = split(u)
     gather(1, u_parts)
     ubuf[...] = u
     halo1 = send_halo(ubuf, 1)
-
-    local_part(u, shifts, hilo, acc)
-    p0 = lane_sum(beta * beta)
-    p1 = lane_sum(beta * u)
-    theta = jnp.where(p0 > 0, p1 / p0, 0.0)
-    e = u - theta * beta
-    q = lane_sum(e * e)
-    t = lane_sum(e * beta)
+    hear(1)
+    tell(2)
 
     slot = {offset: j for j, offset in enumerate(SNP_OFFSETS)}
     lane = lax.broadcasted_iota(jnp.int32, (1, BLK), 1)
@@ -324,6 +350,14 @@
     load_geno.wait()
     partial_scores(0)
 
+    local_part(u, shifts, hilo, acc)
+    p0 = lane_sum(beta * beta)
+    p1 = lane_sum(beta * u)
+    theta = jnp.where(p0 > 0, p1 / p0, 0.0)
+    e = u - theta * beta
+    q = lane_sum(e * e)
+    t = lane_sum(e * beta)
+
     g = off_diagonal(u_parts, 1, halo1) - theta * u
     f = lane_sum(e * g)
     h = lane_sum(beta * g)
@@ -334,6 +368,7 @@
         tile = jnp.where(tile_lane >= 16 * (k + 1), value, tile)
     tile = jnp.where(tile_lane % 16 == tile_row, tile, 0.0)
     sums = jnp.sum(tile, axis=0, keepdims=True)
+    hear(2)
     mom_own[...] = sums
     mom_in[len(SNP_OFFSETS)] = sums
     for j, (dy, dz) in enumerate(SNP_OFFSETS):
@@ -497,6 +532,7 @@
             dma((2, 2)),
             dma((9,)),
             dma((9,)),
+            pltpu.SemaphoreType.REGULAR((3,)),
         ],
         name="ldpred_scores",
         compiler_params=pltpu.CompilerParams(

time: 42.3 us -> 41 us (0.969)
  Pallas kernels: 41.5 us -> 40.2 us
    pallas_call x1, Pallas kernels: 40.1 us -> 38.9 us  [local(): pl.pallas_call(kernel, out_shape=(jax.ShapeDtypeStruct((TR, COLS), F32),...]
where the time goes in v6:
time: 41 us; the launch traced here: 40.9 us
  Pallas kernels  40.2 us (98%)
  between operations  0.64 us (2%)
    pallas_call x1, Pallas kernels, local(): pl.pallas_call(kernel, out_shape=(jax.ShapeDtypeStruct((TR, COLS), F32),...  38.9 us
    pallas_call x1, Pallas kernels, local(): pl.pallas_call(hand_over, out_shape=(jax.ShapeDtypeStruct((TR, COLS), F32...  1.38 us

profile of v6, /device:TPU:1, one launch (start us, length us, event | category | flops | bytes accessed | tf_op | source)
XLA Modules:
  0.0 40.9 jit_solution(14389847228868534790)
XLA Ops:
  0.6 38.9 %ldpred_scores.1 = (f32[8,1024]{1,0:T(8,128)}, f32[32,64]{1,0:T(8,128)}) custom-call(s32[8]{0:T(128)} %start_hbm.1, f32[8]{0:T(128)} %herit_hbm.1, f32[8,1024]{1,0:T(8,128)} %beta_hbm.1, f32[1024,1024]{1,0:T(8,128)} %ld_ref.1, bf16[1024,1024]{1,0:T(8,128)(2,1)} %geno_ref.1), custom_call_target="tpu_custom_call" | custom-call | tf_op jit(solution)/shard_map/ldpred_scores/pallas_call | solution.py:495
  39.5 1.4 %hand_over.1 = (f32[8,1024]{1,0:T(8,128)}, f32[32,64]{1,0:T(8,128)}) custom-call(f32[8,1024]{1,0:T(8,128)} %get-tuple-element.6.weights_ref, f32[32,64]{1,0:T(8,128)} %get-tuple-element.7.scores_ref), custom_call_target="tpu_custom_call" | custom-call | tf_op jit(solution)/shard_map/hand_over/pallas_call | solution.py:542

commit v7 on v6

--- a/solution.py
+++ b/solution.py
@@ -30,10 +30,10 @@
     ((a, b) for a in range(Y) for b in range(Z) if (a, b) != (0, 0)),
     key=lambda q: -(min(q[0], Y - q[0]) + min(q[1], Z - q[1])),
 )
-CHIP_OFFSETS = sorted(
-    ((a, b, c) for a in range(X) for b in range(Y) for c in range(Z) if (a, b, c) != (0, 0, 0)),
-    key=lambda q: -(min(q[0], X - q[0]) + min(q[1], Y - q[1]) + min(q[2], Z - q[2])),
-)
+ALL_OFFSETS = sorted(
+    ((a, b, c, d) for a in range(X) for b in range(Y) for c in range(Z) for d in range(2)),
+    key=lambda q: -(min(q[0], X - q[0]) + min(q[1], Y - q[1]) + min(q[2], Z - q[2])) - q[3] / 2,
+)[:-1]
 IND_OFFSETS = [(a, c) for a in ring(X) for c in (1, 0) if (a, c) != (0, 0)]
 
 
@@ -83,6 +83,10 @@
 
 def wait_for(ref, sem):
     pltpu.make_async_copy(ref, ref, sem).wait()
+
+
+def row_sum(value):
+    return jnp.sum(value, axis=0, keepdims=True)
 
 
 def lane_sum(value):
@@ -139,14 +143,32 @@
     def ind_peer(dx, dc):
         return lax.rem(x + dx, X) * 2 + lax.rem(core + dc, 2)
 
-    near_peers = [(s, i + 1 - 2 * core)]
-    far_peers = [
-        (lax.rem(y + dy, Y) * Z + lax.rem(z + dz, Z), lax.rem(x + dx, X) * 2 + core)
-        for dx, dy, dz in CHIP_OFFSETS
+    everyone = [
+        (snp_peer(dy, dz), ind_peer(dx, dc)) for dx, dy, dz, dc in ALL_OFFSETS
     ]
 
     def load(b):
         return pltpu.make_async_copy(ld_ref.at[pl.ds(b * BLK, BLK)], ldbuf.at[b], ld_sem.at[b])
+
+    barrier = pltpu.get_barrier_semaphore()
+    right, left = lax.rem(s + 1, SNP), lax.rem(s + SNP - 1, SNP)
+    around_z = [(snp_peer(0, 1), i), (snp_peer(0, Z - 1), i)]
+    around_y = [(snp_peer(dy, 0), i) for dy in range(1, Y)]
+    beside = [(s, ind_peer(dx, dc)) for dx, dc in IND_OFFSETS]
+
+    def signal(sem, peer):
+        pl.semaphore_signal(sem, inc=1, device_id=peer, device_id_type=MESH)
+
+    for peer in around_z + around_y + beside:
+        signal(barrier, peer)
+
+    @pl.when(z == Z - 1)
+    def _():
+        signal(barrier, (right, i))
+
+    @pl.when(z == 0)
+    def _():
+        signal(barrier, (left, i))
 
     small = [
         pltpu.make_async_copy(src, dst, small_sem.at[k])
@@ -160,26 +182,6 @@
         load(b).start()
     load_geno = pltpu.make_async_copy(geno_ref, geno, geno_sem)
     load_geno.start()
-
-    barrier = pltpu.get_barrier_semaphore()
-    right, left = lax.rem(s + 1, SNP), lax.rem(s + SNP - 1, SNP)
-    around_z = [(snp_peer(0, 1), i), (snp_peer(0, Z - 1), i)]
-    around_y = [(snp_peer(dy, 0), i) for dy in range(1, Y)]
-    beside = [(s, ind_peer(dx, dc)) for dx, dc in IND_OFFSETS]
-
-    def signal(sem, peer):
-        pl.semaphore_signal(sem, inc=1, device_id=peer, device_id_type=MESH)
-
-    for peer in around_z + around_y + beside:
-        signal(barrier, peer)
-
-    @pl.when(z == Z - 1)
-    def _():
-        signal(barrier, (right, i))
-
-    @pl.when(z == 0)
-    def _():
-        signal(barrier, (left, i))
 
     ends = jnp.where(lax.rem(z + 1, Z) < 2, 1, 0)
     pl.semaphore_wait(barrier, len(around_z + around_y + beside) + ends)
@@ -370,11 +372,11 @@
     sums = jnp.sum(tile, axis=0, keepdims=True)
     hear(2)
     mom_own[...] = sums
-    mom_in[len(SNP_OFFSETS)] = sums
+    mom_in[SNP - 1 :] = sums
     for j, (dy, dz) in enumerate(SNP_OFFSETS):
         pltpu.make_async_remote_copy(
             src_ref=mom_own,
-            dst_ref=mom_in.at[j],
+            dst_ref=mom_in.at[pl.ds(j, 1)],
             send_sem=send_sem.at[4],
             recv_sem=recv_sem.at[4],
             device_id=(snp_peer(dy, dz), i),
@@ -394,16 +396,14 @@
     wait_for(mom_in.at[0 : len(SNP_OFFSETS)], recv_sem.at[4])
     moments = mom_in[...]
     p0_d, th_d, q_d, t_d, f_d, h_d = [
-        moments if k == 0 else pltpu.roll(moments, BLK - 16 * k, 2) for k in range(6)
+        moments if k == 0 else pltpu.roll(moments, BLK - 16 * k, 1) for k in range(6)
     ]
-    p0 = jnp.sum(p0_d, axis=0)
-    theta = jnp.sum(p0_d * th_d + t_d, axis=0) / p0
-    delta = th_d - theta[None]
-    q = jnp.sum(q_d + delta * (2.0 * t_d + delta * p0_d), axis=0)
-    t = jnp.sum(t_d + delta * p0_d, axis=0)
-    f = jnp.sum(
-        f_d + delta * (q_d + th_d * t_d + h_d + delta * (t_d + th_d * p0_d)), axis=0
-    )
+    p0 = row_sum(p0_d)
+    theta = row_sum(p0_d * th_d + t_d) / p0
+    delta = th_d - theta
+    q = row_sum(q_d + delta * (2.0 * t_d + delta * p0_d))
+    t = row_sum(t_d + delta * p0_d)
+    f = row_sum(f_d + delta * (q_d + th_d * t_d + h_d + delta * (t_d + th_d * p0_d)))
     a11 = p0 * (theta + kappa)
     a12 = q + (theta + kappa) * t
     a22 = f + kappa * q
@@ -415,11 +415,11 @@
     coef = jnp.where(own_lanes, c0, 0.0) + pltpu.roll(jnp.where(own_lanes, c1, 0.0), 64, 1)
     coef = pltpu.roll(coef, i * TR, 1)
     coef_own[...] = coef
-    coef_in[len(IND_OFFSETS)] = coef
+    coef_in[IND - 1 :] = coef
     for j, (dx, dc) in enumerate(IND_OFFSETS):
         pltpu.make_async_remote_copy(
             src_ref=coef_own,
-            dst_ref=coef_in.at[j],
+            dst_ref=coef_in.at[pl.ds(j, 1)],
             send_sem=send_sem.at[5],
             recv_sem=recv_sem.at[5],
             device_id=(s, ind_peer(dx, dc)),
@@ -437,7 +437,7 @@
 
     beta_scores = total_scores(0)
     wait_for(coef_in.at[0 : len(IND_OFFSETS)], recv_sem.at[5])
-    coef = jnp.sum(coef_in[...], axis=0)
+    coef = row_sum(coef_in[...])
     swapped = pltpu.roll(coef, 64, 1)
     beta_scores = beta_scores * jnp.where(half, coef, swapped)
     raw = beta_scores + total_scores(1) * jnp.where(half, swapped, coef)
@@ -445,30 +445,28 @@
     mean = both(jnp.sum(raw, axis=0, keepdims=True)) * (1.0 / SHARE)
     spread = both(jnp.sum((raw - mean) * (raw - mean), axis=0, keepdims=True))
     stat = jnp.where(half, mean, spread)
-    size = SHARE
-    for turn, peers in enumerate((near_peers, far_peers)):
-        count = len(peers) + 1
-        stat_own[turn] = stat
-        stat_in[turn, len(peers)] = stat
-        for j, peer in enumerate(peers):
-            pltpu.make_async_remote_copy(
-                src_ref=stat_own.at[turn],
-                dst_ref=stat_in.at[turn, j],
-                send_sem=send_sem.at[6 + turn],
-                recv_sem=recv_sem.at[6 + turn],
-                device_id=peer,
-                device_id_type=MESH,
-            ).start()
-        arrived = stat_in.at[turn, 0 : len(peers)]
-        pending.append(lambda turn=turn, arrived=arrived: wait_for(arrived, send_sem.at[6 + turn]))
-        wait_for(arrived, recv_sem.at[6 + turn])
-        values = stat_in[turn, 0:count]
-        total = jnp.sum(values, axis=0)
-        mean = total * (1.0 / count)
-        apart = jnp.where(half, values - mean, 0.0)
-        squares = jnp.sum(apart * apart, axis=0) * float(size)
-        stat = jnp.where(half, mean, total + pltpu.roll(squares, 64, 1))
-        size *= count
+    count = len(everyone) + 1
+    stat_own[...] = stat
+    stat_in[len(everyone) :] = stat
+    for j, peer in enumerate(everyone):
+        pltpu.make_async_remote_copy(
+            src_ref=stat_own,
+            dst_ref=stat_in.at[pl.ds(j, 1)],
+            send_sem=send_sem.at[6],
+            recv_sem=recv_sem.at[6],
+            device_id=peer,
+            device_id_type=MESH,
+        ).start()
+    arrived = stat_in.at[0 : len(everyone)]
+    pending.append(lambda: wait_for(arrived, send_sem.at[6]))
+    wait_for(arrived, recv_sem.at[6])
+    values = stat_in[...]
+    total = row_sum(values)
+    mean = total * (1.0 / count)
+    apart = jnp.where(half, values - mean, 0.0)
+    squares = row_sum(apart * apart) * float(SHARE)
+    stat = jnp.where(half, mean, total + pltpu.roll(squares, 64, 1))
+    size = SHARE * count
     swapped = pltpu.roll(stat, 64, 1)
     mean = jnp.where(half, stat, swapped)
     variance = jnp.where(half, swapped, stat) * (1.0 / size)
@@ -512,16 +510,16 @@
             pltpu.VMEM((2, 2, TR, HALO), F32),
             pltpu.VMEM((2, IND, 16, COLS), BF16),
             pltpu.VMEM((1, BLK), F32),
-            pltpu.VMEM((SNP, 1, BLK), F32),
+            pltpu.VMEM((SNP, BLK), F32),
             pltpu.VMEM((1, BLK), F32),
-            pltpu.VMEM((IND, 1, BLK), F32),
+            pltpu.VMEM((IND, BLK), F32),
             pltpu.VMEM((2, SNP, 16, BLK), F32),
             pltpu.VMEM((SNP - 1, 16, BLK), F32),
             pltpu.VMEM((Y - 1, Z, 16, BLK), F32),
             pltpu.VMEM((Z, 16, BLK), F32),
             pltpu.VMEM((Z - 1, 16, BLK), F32),
-            pltpu.VMEM((2, 1, BLK), F32),
-            pltpu.VMEM((2, X * Y * Z, 1, BLK), F32),
+            pltpu.VMEM((1, BLK), F32),
+            pltpu.VMEM((SNP * IND, BLK), F32),
             pltpu.VMEM((TR, COLS), F32),
             pltpu.VMEM((SHARE, 64), F32),
             dma((NB,)),

time: 41 us -> 40.1 us (0.978)
  Pallas kernels: 40.2 us -> 39.4 us
    pallas_call x1, Pallas kernels: 38.9 us -> 38 us  [local(): pl.pallas_call(kernel, out_shape=(jax.ShapeDtypeStruct((TR, COLS), F32),...]
where the time goes in v7:
time: 40.1 us; the launch traced here: 40 us
  Pallas kernels  39.4 us (98%)
  between operations  0.64 us (2%)
    pallas_call x1, Pallas kernels, local(): pl.pallas_call(kernel, out_shape=(jax.ShapeDtypeStruct((TR, COLS), F32),...  38 us
    pallas_call x1, Pallas kernels, local(): pl.pallas_call(hand_over, out_shape=(jax.ShapeDtypeStruct((TR, COLS), F32...  1.38 us

profile of v7, /device:TPU:1, one launch (start us, length us, event | category | flops | bytes accessed | tf_op | source)
XLA Modules:
  0.0 40.0 jit_solution(4914290726318947559)
XLA Ops:
  0.6 38.0 %ldpred_scores.1 = (f32[8,1024]{1,0:T(8,128)}, f32[32,64]{1,0:T(8,128)}) custom-call(s32[8]{0:T(128)} %start_hbm.1, f32[8]{0:T(128)} %herit_hbm.1, f32[8,1024]{1,0:T(8,128)} %beta_hbm.1, f32[1024,1024]{1,0:T(8,128)} %ld_ref.1, bf16[1024,1024]{1,0:T(8,128)(2,1)} %geno_ref.1), custom_call_target="tpu_custom_call" | custom-call | tf_op jit(solution)/shard_map/ldpred_scores/pallas_call | solution.py:493
  38.6 1.4 %hand_over.1 = (f32[8,1024]{1,0:T(8,128)}, f32[32,64]{1,0:T(8,128)}) custom-call(f32[8,1024]{1,0:T(8,128)} %get-tuple-element.6.weights_ref, f32[32,64]{1,0:T(8,128)} %get-tuple-element.7.scores_ref), custom_call_target="tpu_custom_call" | custom-call | tf_op jit(solution)/shard_map/hand_over/pallas_call | solution.py:540

commit v8 on v7

--- a/solution.py
+++ b/solution.py
@@ -407,9 +407,10 @@
     a11 = p0 * (theta + kappa)
     a12 = q + (theta + kappa) * t
     a22 = f + kappa * q
-    det = a11 * a22 - a12 * a12
-    c1 = jnp.where(det > 0, (t * a11 - p0 * a12) / det, 0.0)
-    c0 = (p0 - c1 * a12) / a11 - c1 * theta
+    ratio = a12 / a11
+    rest = a22 - a12 * ratio
+    c1 = jnp.where(rest > 0, (t - p0 * ratio) / rest, 0.0)
+    c0 = p0 / a11 - c1 * (ratio + theta)
 
     own_lanes = lane < TR
     coef = jnp.where(own_lanes, c0, 0.0) + pltpu.roll(jnp.where(own_lanes, c1, 0.0), 64, 1)

time: 40.1 us -> 40.1 us (level)
  no operation moved by 1% of the time
where the time goes in v8:
time: 40.1 us; the launch traced here: 40 us
  Pallas kernels  39.3 us (98%)
  between operations  0.64 us (2%)
    pallas_call x1, Pallas kernels, local(): pl.pallas_call(kernel, out_shape=(jax.ShapeDtypeStruct((TR, COLS), F32),...  38 us
    pallas_call x1, Pallas kernels, local(): pl.pallas_call(hand_over, out_shape=(jax.ShapeDtypeStruct((TR, COLS), F32...  1.38 us

profile of v8, /device:TPU:1, one launch (start us, length us, event | category | flops | bytes accessed | tf_op | source)
XLA Modules:
  0.0 40.0 jit_solution(8599621311581393378)
XLA Ops:
  0.6 38.0 %ldpred_scores.1 = (f32[8,1024]{1,0:T(8,128)}, f32[32,64]{1,0:T(8,128)}) custom-call(s32[8]{0:T(128)} %start_hbm.1, f32[8]{0:T(128)} %herit_hbm.1, f32[8,1024]{1,0:T(8,128)} %beta_hbm.1, f32[1024,1024]{1,0:T(8,128)} %ld_ref.1, bf16[1024,1024]{1,0:T(8,128)(2,1)} %geno_ref.1), custom_call_target="tpu_custom_call" | custom-call | tf_op jit(solution)/shard_map/ldpred_scores/pallas_call | solution.py:494
  38.6 1.4 %hand_over.1 = (f32[8,1024]{1,0:T(8,128)}, f32[32,64]{1,0:T(8,128)}) custom-call(f32[8,1024]{1,0:T(8,128)} %get-tuple-element.6.weights_ref, f32[32,64]{1,0:T(8,128)} %get-tuple-element.7.scores_ref), custom_call_target="tpu_custom_call" | custom-call | tf_op jit(solution)/shard_map/hand_over/pallas_call | solution.py:541

commit v9 on v8

--- a/solution.py
+++ b/solution.py
@@ -460,6 +460,9 @@
         ).start()
     arrived = stat_in.at[0 : len(everyone)]
     pending.append(lambda: wait_for(arrived, send_sem.at[6]))
+    for drain in pending:
+        drain()
+    store_weights.wait()
     wait_for(arrived, recv_sem.at[6])
     values = stat_in[...]
     total = row_sum(values)
@@ -476,10 +479,6 @@
     scores_ref[16:32, :] = scores[:, 64:128]
     store_scores = pltpu.make_async_copy(scores_ref, scores_out, out_sem.at[1])
     store_scores.start()
-
-    for drain in pending:
-        drain()
-    store_weights.wait()
     store_scores.wait()
 
 

time: 40.1 us -> 40.1 us (level)
  no operation moved by 1% of the time
where the time goes in v9:
time: 40.1 us; the launch traced here: 40 us
  Pallas kernels  39.3 us (98%)
  between operations  0.64 us (2%)
    pallas_call x1, Pallas kernels, local(): pl.pallas_call(kernel, out_shape=(jax.ShapeDtypeStruct((TR, COLS), F32),...  38 us
    pallas_call x1, Pallas kernels, local(): pl.pallas_call(hand_over, out_shape=(jax.ShapeDtypeStruct((TR, COLS), F32...  1.38 us

profile of v9, /device:TPU:1, one launch (start us, length us, event | category | flops | bytes accessed | tf_op | source)
XLA Modules:
  0.0 40.0 jit_solution(10303220807276170847)
XLA Ops:
  0.6 38.0 %ldpred_scores.1 = (f32[8,1024]{1,0:T(8,128)}, f32[32,64]{1,0:T(8,128)}) custom-call(s32[8]{0:T(128)} %start_hbm.1, f32[8]{0:T(128)} %herit_hbm.1, f32[8,1024]{1,0:T(8,128)} %beta_hbm.1, f32[1024,1024]{1,0:T(8,128)} %ld_ref.1, bf16[1024,1024]{1,0:T(8,128)(2,1)} %geno_ref.1), custom_call_target="tpu_custom_call" | custom-call | tf_op jit(solution)/shard_map/ldpred_scores/pallas_call | solution.py:493
  38.6 1.4 %hand_over.1 = (f32[8,1024]{1,0:T(8,128)}, f32[32,64]{1,0:T(8,128)}) custom-call(f32[8,1024]{1,0:T(8,128)} %get-tuple-element.6.weights_ref, f32[32,64]{1,0:T(8,128)} %get-tuple-element.7.scores_ref), custom_call_target="tpu_custom_call" | custom-call | tf_op jit(solution)/shard_map/hand_over/pallas_call | solution.py:540
